TPU v7x, 32 devices: a whole 2x2x4 slice. The times are simulated.
32 devices in a mesh: window: 16 (over z, x, core), token: 2 (over y).
Axes of the slice: x: 2, y: 2, z: 4, core: 2. Of those that a mesh axis runs over, the one named last changes fastest.
Arguments:
- latents: bfloat16 [16, 9, 32, 5120], P('window', None, 'token'), may hold values from -36 to 36
- queries: bfloat16 [16, 9, 32, 5120], P('window', None, 'token'), may hold values from -128 to 128
- attn_keys: bfloat16 [16, 9, 32, 5120], P('window', None, 'token'), may hold values from -4.5 to 4.5
- cached: bfloat16 [4, 16, 9, 32, 5120], P(None, 'window', None, 'token'), may hold values from -3 to 3
- plan: int32 [4], replicated, may hold values from 0 to 1
- refresh: int32 [16], replicated, may hold values from 0 to 3
- value_gain: float32 [5120], replicated, may hold values from 0.1 to 1.9
- attn_gate: float32 [5120], replicated, may hold values from 0.5 to 3
- intersections: int32 [16], replicated, may hold values from 1 to 4, as said below
Outputs:
- looped: bfloat16 [16, 9, 32, 5120], P('window', None, 'token')
Inputs may be any that keep to these rules, and one draw needn't show every extreme that they name: `intersections`: some window has exactly 4.
All inputs are finite; a program needn't handle non-finite values.
Results may differ from a plain program's by a relative error of at most 0.0065.
Values may be sent and summed in bfloat16 or wider, within the bound.
A program may use at most 128 MiB of HBM per device.

v0:
```python
import math

import jax
import jax.numpy as jnp
from jax import lax
from jax.sharding import PartitionSpec as P

HEAD_DIM = 128
MAXOV = 4


def from_behind(value, axis, steps):
    count = lax.axis_size(axis)
    pairs = [(source, (source + steps) % count) for source in range(count)]
    return lax.ppermute(value, axis, pairs)


def on_device(
    latents, queries, attn_keys, cached, plan, refresh, value_gain, attn_gate, intersections
):
    frames = latents.shape[1]
    spots = latents.shape[2]
    width = latents.shape[3]
    depth = HEAD_DIM
    heads = width // depth
    inv_root = 1.0 / math.sqrt(depth)
    window_id = lax.axis_index("window")
    windows_here = lax.axis_size("window")
    slots = jnp.arange(windows_here)
    chosen = jnp.sum(jnp.where(slots == window_id, refresh, 0))
    block_ids = jnp.arange(cached.shape[0])
    mix_before = jnp.where(block_ids < chosen, plan, 0).astype(jnp.bfloat16)
    mix_after = jnp.where(block_ids > chosen, plan, 0).astype(jnp.bfloat16)
    stack = cached[:, 0]
    hidden = latents[0].astype(jnp.float32) + jnp.einsum(
        "b,bfsd->fsd", mix_before, stack, preferred_element_type=jnp.float32
    )
    mean_square = jnp.mean(hidden * hidden, axis=-1, keepdims=True)
    values = (hidden / jnp.sqrt(mean_square + 1e-06) * value_gain).astype(jnp.bfloat16)
    own_queries = queries[0]
    own_keys = attn_keys[0]
    rows = frames * spots
    query_rows = own_queries.reshape(rows, heads, depth)
    running = jnp.full((heads, rows), -jnp.inf, jnp.float32)
    summed = jnp.zeros((heads, rows), jnp.float32)
    accum = jnp.zeros((heads, rows, depth), jnp.float32)
    key_rows = lax.all_gather(own_keys, "token", axis=1, tiled=True).reshape(-1, heads, depth)
    value_rows = lax.all_gather(values, "token", axis=1, tiled=True).reshape(-1, heads, depth)
    scores = (
        jnp.einsum("qhd,khd->hqk", query_rows, key_rows, preferred_element_type=jnp.float32)
        * inv_root
    )
    peak = jnp.max(scores, axis=-1)
    weights = jnp.exp(scores - peak[:, :, None])
    fade = jnp.exp(running - peak)
    summed = summed * fade + jnp.sum(weights, axis=-1)
    accum = accum * fade[:, :, None] + jnp.einsum(
        "hqk,khd->hqd", weights.astype(jnp.bfloat16), value_rows, preferred_element_type=jnp.float32
    )
    running, summed, accum = (peak, summed, accum)
    attended = (accum / summed[:, :, None]).astype(jnp.bfloat16)
    attended = jnp.transpose(attended, (1, 0, 2)).reshape(frames, spots, width)
    later = hidden + jnp.einsum("b,bfsd->fsd", mix_after, stack, preferred_element_type=jnp.float32)
    pre = (later + attn_gate * attended.astype(jnp.float32)).astype(jnp.bfloat16)
    from_prev = from_behind(pre[frames - MAXOV :], "window", 1)
    from_next = from_behind(pre[:MAXOV], "window", -1)
    ov_next = jnp.sum(jnp.where(slots == window_id, intersections, 0))
    ov_prev = jnp.sum(
        jnp.where(slots == (window_id + windows_here - 1) % windows_here, intersections, 0)
    )
    frame_ids = jnp.arange(frames)
    slab_ids = jnp.arange(MAXOV)
    tail_pos = frame_ids - (frames - ov_next)
    in_tail = tail_pos >= 0
    in_head = frame_ids < ov_prev
    pick_next = ((slab_ids[None, :] == tail_pos[:, None]) & in_tail[:, None]).astype(jnp.bfloat16)
    pick_prev = (
        (slab_ids[None, :] == (MAXOV - ov_prev + frame_ids)[:, None]) & in_head[:, None]
    ).astype(jnp.bfloat16)
    partner_next = jnp.einsum(
        "fs,spd->fpd", pick_next, from_next, preferred_element_type=jnp.float32
    )
    partner_prev = jnp.einsum(
        "fs,spd->fpd", pick_prev, from_prev, preferred_element_type=jnp.float32
    )
    mine = pre.astype(jnp.float32)
    ramp_tail = ((tail_pos + 1).astype(jnp.float32) / (ov_next + 1).astype(jnp.float32))[
        :, None, None
    ]
    ramp_head = ((frame_ids + 1).astype(jnp.float32) / (ov_prev + 1).astype(jnp.float32))[
        :, None, None
    ]
    tail_mix = (1.0 - ramp_tail) * mine + ramp_tail * partner_next
    head_mix = (1.0 - ramp_head) * partner_prev + ramp_head * mine
    looped = jnp.where(
        in_tail[:, None, None], tail_mix, jnp.where(in_head[:, None, None], head_mix, mine)
    )
    return looped.astype(jnp.bfloat16)[None]


def solution(mesh):
    in_specs = (
        P("window", None, "token", None),
        P("window", None, "token", None),
        P("window", None, "token", None),
        P(None, "window", None, "token", None),
        P(),
        P(),
        P(),
        P(),
        P(),
    )
    out_specs = P("window", None, "token", None)
    return jax.shard_map(
        on_device, mesh=mesh, in_specs=in_specs, out_specs=out_specs, check_vma=False
    )
```

profile of v0, /device:TPU:0, one launch (start us, length us, event | category | flops | bytes accessed | tf_op | source)
XLA Modules:
  0.0 176.0 jit_solution(16022385421515422321)
XLA Ops:
  6.5 1.3 fusion.38
  7.9 8.4 %fusion.11 = f32[1,9,16,5120]{3,0,2,1:T(1,128)S(1)} fusion(bf16[4,9,16,5120]{3,2,1,0:T(8,128)(2,1)} %bitcast.71, s32[4]{0:T(128)} %param.13, s32[]{:T(128)} %get-tuple-element.13), kind=kOutput, calls=%fused_computation.23 | convolution fusion | flops 5898252 | bytes 8847380 | tf_op jit(solution)/shard_map/b,bfsd->fsd/dot_general | solution.py:35
  16.3 0.0 copy-start
  16.3 0.0 copy-start.5
  16.3 4.7 %multiply_reduce_fusion.1 = f32[9,16]{0,1:T(8,128)S(1)} fusion(f32[1,9,16,5120]{3,0,2,1:T(1,128)S(1)} %fusion.11, bf16[1,9,16,5120]{3,2,1,0:T(8,128)(2,1)} %param.9), kind=kLoop, calls=%fused_computation.20 | loop fusion | flops 2948976 | bytes 4424256 | tf_op jit(solution)/shard_map/reduce_sum | solution.py:38
  21.0 2.6 %multiply_convert_fusion = bf16[9,16,5120]{2,0,1:T(8,128)(2,1)S(1)} fusion(f32[1,9,16,5120]{3,0,2,1:T(1,128)S(1)} %fusion.11, bf16[1,9,16,5120]{3,2,1,0:T(8,128)(2,1)S(1)} %copy-done, f32[5120]{0:T(1024)S(1)} %copy-done.5, f32[9,16]{0,1:T(8,128)S(1)} %add_sqrt_fusion), kind=kLoop, calls=%fused_computation.19 | loop fusion | flops 3686400 | bytes 5919296 | tf_op jit(solution)/shard_map/convert_element_type | solution.py:39
  23.7 0.0 copy-start.7
  23.7 2.2 %copy.24 = bf16[9,16,5120]{2,1,0:T(8,128)(2,1)} copy(bf16[9,16,5120]{2,0,1:T(8,128)(2,1)S(1)} %multiply_convert_fusion) | data formatting | bytes 2949120 | tf_op jit(solution)/shard_map/convert_element_type | solution.py:39
  25.9 0.0 all-gather.4.cloned.1.call-update
  26.0 0.0 all-gather.6.cloned.1.call-start
  26.0 0.7 all-gather.6.cloned.1.call-update
  26.7 2.7 %copy.34 = bf16[18,8,40,128]{3,2,1,0:T(8,128)(2,1)} copy(bf16[18,8,40,128]{3,1,2,0:T(8,128)(2,1)} %bitcast.70) | data formatting | bytes 2949120
  30.7 10.0 %fusion.9 = f32[1,9,16,5120]{3,0,2,1:T(1,128)} fusion(bf16[4,9,16,5120]{3,2,1,0:T(8,128)(2,1)} %bitcast.72, s32[4]{0:T(128)S(1)} %copy-done.7, s32[]{:T(128)} %get-tuple-element.13), kind=kOutput, calls=%fused_computation.21 | convolution fusion | flops 5898252 | bytes 8847380 | tf_op jit(solution)/shard_map/b,bfsd->fsd/dot_general | solution.py:63
  40.7 30.9 %all-gather.4.cloned.1.call-done = bf16[9,32,5120]{2,1,0:T(8,128)(2,1)} async-done(((bf16[9,16,5120]{2,1,0:T(8,128)(2,1)}), bf16[9,32,5120]{2,1,0:T(8,128)(2,1)}) %all-gather.4.cloned.1.call-update) | async-done | bytes 2949136 | tf_op jit(solution)/shard_map/all_gather | solution.py:48
  71.5 4.0 %copy.36 = bf16[36,8,40,128]{3,2,1,0:T(8,128)(2,1)} copy(bf16[36,8,40,128]{3,1,2,0:T(8,128)(2,1)} %bitcast.67) | data formatting | bytes 5898240
  75.5 40.3 %all-gather.6.cloned.1.call-done = bf16[1,9,32,5120]{3,2,1,0:T(8,128)(2,1)} async-done(((bf16[1,9,16,5120]{3,2,1,0:T(8,128)(2,1)}), bf16[1,9,32,5120]{3,2,1,0:T(8,128)(2,1)}) %all-gather.6.cloned.1.call-update) | async-done | bytes 2949136 | tf_op jit(solution)/shard_map/all_gather | solution.py:47
  115.8 2.4 %copy.35 = bf16[36,8,40,128]{3,2,1,0:T(8,128)(2,1)S(1)} copy(bf16[36,8,40,128]{3,1,2,0:T(8,128)(2,1)} %bitcast.68) | data formatting | bytes 5898240
  118.3 1.8 %multiply_reduce_fusion = (f32[40,144]{1,0:T(8,128)S(1)}, f32[40,144,288]{2,1,0:T(8,128)S(1)}) fusion(bf16[288,40,128]{2,1,0:T(8,128)(2,1)S(1)} %bitcast.65, bf16[144,40,128]{2,1,0:T(8,128)(2,1)S(1)} %bitcast.66), kind=kOutput, calls=%fused_computation.1 | convolution fusion | flops 427985280 | bytes 11082240 | tf_op jit(solution)/shard_map/qhd,khd->hqk/dot_general | solution.py:50
  120.1 3.2 %fusion = f32[40,144]{1,0:T(8,128)S(1)} fusion(f32[40,144,288]{2,1,0:T(8,128)S(1)} %get-tuple-element.12, f32[40,144]{1,0:T(8,128)S(1)} %get-tuple-element.11), kind=kLoop, calls=%fused_computation.5 | loop fusion | flops 4970880 | bytes 6681600 | tf_op jit(solution)/shard_map/reduce_sum | solution.py:56
  123.4 4.0 %fusion.22 = f32[144,40,128]{2,0,1:T(8,128)S(1)} fusion(f32[144,40]{0,1:T(8,128)S(1)} %bitcast_add_fusion.2, f32[144,40]{0,1:T(8,128)S(1)} %multiply_bitcast_fusion, bf16[288,40,128]{2,1,0:T(8,128)(2,1)S(1)} %bitcast.69, f32[40,144,288]{2,1,0:T(8,128)S(1)} %get-tuple-element.12, f32[40,144]{1,0:T(8,128)S(1)} %get-tuple-element.11), kind=kOutput, calls=%fused_computation.34 | convolution fusion | flops 432599040 | bytes 12602880 | tf_op jit(solution)/shard_map/hqk,khd->hqd/dot_general | solution.py:57
  127.4 2.6 %copy.26 = f32[144,40,128]{2,1,0:T(8,128)} copy(f32[144,40,128]{2,0,1:T(8,128)S(1)} %fusion.22) | data formatting | bytes 5898240 | tf_op jit(solution)/shard_map/convert_element_type | solution.py:64
  129.9 4.1 %reshape.78 = f32[9,16,5120]{2,1,0:T(8,128)} reshape(f32[144,40,128]{2,1,0:T(8,128)} %copy.26) | data formatting | bytes 5898240 | tf_op jit(solution)/shard_map/convert_element_type | solution.py:64
  134.0 10.0 %fusion.8 = bf16[9,16,5120]{2,0,1:T(8,128)(2,1)S(1)} fusion(f32[1,9,16,5120]{3,0,2,1:T(1,128)} %fusion.9, f32[9,16,5120]{2,1,0:T(8,128)} %reshape.78, f32[1,9,16,5120]{3,0,2,1:T(1,128)S(1)} %fusion.11, bf16[1,9,16,5120]{3,2,1,0:T(8,128)(2,1)} %param.9, f32[5120]{0:T(1024)S(1)} %copy-done.6), kind=kLoop, calls=%fused_computation.17 | loop fusion | flops 4423680 | bytes 11816960 | tf_op jit(solution)/shard_map/convert_element_type | solution.py:64
  144.0 1.5 copy-done.2
  145.5 1.3 fusion.56
  146.9 0.0 collective-permute-start.1
  146.9 0.8 iota_compare_fusion.2
  147.7 4.6 %collective-permute-start = (bf16[4,16,5120]{2,0,1:T(4,128)(2,1)S(1)}, bf16[4,16,5120]{2,0,1:T(4,128)(2,1)}, u32[]{:S(2)}, u32[]{:S(2)}) collective-permute-start(bf16[4,16,5120]{2,0,1:T(4,128)(2,1)S(1)} %get-tuple-element.9), channel_id=1, source_target_pairs={{0,30},{2,0},{4,2},{6,4},{8,6},{10,8},{12,10},{14,12},{16,14},{18,... | collective-permute-start | bytes 1966088 | tf_op jit(solution)/shard_map/ppermute | solution.py:15
  153.5 6.5 %collective-permute-done.1 = bf16[4,16,5120]{2,0,1:T(4,128)(2,1)} collective-permute-done((bf16[4,16,5120]{2,0,1:T(4,128)(2,1)}, bf16[4,16,5120]{2,0,1:T(4,128)(2,1)}, u32[]{:S(2)}, u32[]{:S(2)}) %collective-permute-start.1) | collective-permute-done | bytes 655392 | tf_op jit(solution)/shard_map/ppermute | solution.py:15
  160.0 4.0 %convert_select_fusion = bf16[9,16,5120]{2,0,1:T(8,128)(2,1)S(1)} fusion(bf16[9,16,5120]{2,0,1:T(8,128)(2,1)} %copy-done.2, bf16[4,16,5120]{2,0,1:T(4,128)(2,1)} %collective-permute-done.1, f32[9]{0:T(128)S(1)} %convert_divide_fusion, f32[9]{0:T(128)S(1)} %broadcast_subtract_fusion, pred[9]{0:T(512)(128)(4,1)S(1)} %iota_compare_fusion.2, s32[9]{0:T(128)S(1)} %iota_add_fusion), kind=kOutput, calls=%fused_computation.2 | convolution fusion | flops 9584712 | bytes 3604597 | tf_op jit(solution)/shard_map/fs,spd->fpd/dot_general | solution.py:83
  164.0 3.2 %fusion.6 = bf16[1,9,16,5120]{3,1,2,0:T(8,128)(2,1)S(1)} fusion(bf16[9,16,5120]{2,0,1:T(8,128)(2,1)S(1)} %convert_select_fusion, bf16[4,16,5120]{2,0,1:T(4,128)(2,1)} %collective-permute-done, bf16[9,16,5120]{2,0,1:T(8,128)(2,1)S(1)} %copy-done.3, f32[9]{0:T(128)S(1)} %get-tuple-element.8, f32[9]{0:T(128)S(1)} %get-tuple-element.7, ...), kind=kOutput, calls=%fused_computation.13 | convolution fusion | flops 9584712 | bytes 5079157 | tf_op jit(solution)/shard_map/fs,spd->fpd/dot_general | solution.py:80
  167.2 2.0 %copy.28 = bf16[1,9,16,5120]{3,2,1,0:T(8,128)(2,1)} copy(bf16[1,9,16,5120]{3,1,2,0:T(8,128)(2,1)S(1)} %fusion.6) | data formatting | bytes 2949120 | tf_op jit(solution)/shard_map/broadcast_in_dim | solution.py:98
  (23 shorter events, 0.1 us)
Async XLA Ops:
  6.5 65.0 %all-gather.4.cloned.1.call-start = ((), (), s32[]{:S(2)}) async-start(), calls=%async_computation | async-start | bytes 4423680 | tf_op jit(solution)/shard_map/all_gather | solution.py:48
  16.3 4.7 %copy-start = (bf16[1,9,16,5120]{3,2,1,0:T(8,128)(2,1)S(1)}, bf16[1,9,16,5120]{3,2,1,0:T(8,128)(2,1)}, u32[]{:S(2)}) copy-start(bf16[1,9,16,5120]{3,2,1,0:T(8,128)(2,1)} %param.9) | copy-start | bytes 4423684
  16.3 4.7 %copy-start.5 = (f32[5120]{0:T(1024)S(1)}, f32[5120]{0:T(1024)}, u32[]{:S(2)}) copy-start(f32[5120]{0:T(1024)} %param.15) | copy-start | bytes 61444
  23.7 7.0 %copy-start.7 = (s32[4]{0:T(128)S(1)}, s32[4]{0:T(128)}, u32[]{:S(2)}) copy-start(s32[4]{0:T(128)} %param.13) | copy-start | bytes 52
  26.0 89.9 %all-gather.6.cloned.1.call-start = ((), (), s32[]{:S(2)}) async-start(), calls=%async_computation.1 | async-start | bytes 4423680 | tf_op jit(solution)/shard_map/all_gather | solution.py:47
  115.8 2.5 %copy-start.1 = (bf16[18,8,40,128]{3,2,1,0:T(8,128)(2,1)S(1)}, bf16[18,8,40,128]{3,2,1,0:T(8,128)(2,1)}, u32[]{:S(2)}) copy-start(bf16[18,8,40,128]{3,2,1,0:T(8,128)(2,1)} %copy.34) | copy-start | bytes 4423684
  120.1 3.2 %copy-start.4 = (bf16[36,8,40,128]{3,2,1,0:T(8,128)(2,1)S(1)}, bf16[36,8,40,128]{3,2,1,0:T(8,128)(2,1)}, u32[]{:S(2)}) copy-start(bf16[36,8,40,128]{3,2,1,0:T(8,128)(2,1)} %copy.36) | copy-start | bytes 8847364
  129.9 4.1 %copy-start.6 = (f32[5120]{0:T(1024)S(1)}, f32[5120]{0:T(1024)}, u32[]{:S(2)}) copy-start(f32[5120]{0:T(1024)} %param.16) | copy-start | bytes 61444
  144.0 1.5 copy-start.2
  146.9 17.1 %copy-start.3 = (bf16[9,16,5120]{2,0,1:T(8,128)(2,1)S(1)}, bf16[9,16,5120]{2,0,1:T(8,128)(2,1)}, u32[]{:S(2)}) copy-start(bf16[9,16,5120]{2,0,1:T(8,128)(2,1)} %copy-done.2) | copy-start | bytes 4423684
  146.9 13.1 %collective-permute-start.1 = (bf16[4,16,5120]{2,0,1:T(4,128)(2,1)}, bf16[4,16,5120]{2,0,1:T(4,128)(2,1)}, u32[]{:S(2)}, u32[]{:S(2)}) collective-permute-start(bf16[4,16,5120]{2,0,1:T(4,128)(2,1)} %get-tuple-element.10), channel_id=1, source_target_pairs={{0,2},{2,4},{4,6},{6,8},{8,10},{10,12},{12,14},{14,16},{16,18},{18... | collective-permute-start | bytes 1966088 | tf_op jit(solution)/shard_map/ppermute | solution.py:15
  147.7 16.3 %collective-permute-start = (bf16[4,16,5120]{2,0,1:T(4,128)(2,1)S(1)}, bf16[4,16,5120]{2,0,1:T(4,128)(2,1)}, u32[]{:S(2)}, u32[]{:S(2)}) collective-permute-start(bf16[4,16,5120]{2,0,1:T(4,128)(2,1)S(1)} %get-tuple-element.9), channel_id=1, source_target_pairs={{0,30},{2,0},{4,2},{6,4},{8,6},{10,8},{12,10},{14,12},{16,14},{18,... | collective-permute-start | bytes 1966088 | tf_op jit(solution)/shard_map/ppermute | solution.py:15
Sparse Core Ops, SparseCore 0:
  26.1 45.4 all-gather.3
  73.1 42.7 all-gather.5
where the time goes:
time: 179 us; the launch traced here: 176 us
  waiting for transfers between devices  78.4 us (44%)
  matrix products  31.4 us (18%)
  local copies, waits for them, and re-layouts  22.9 us (13%)
  other arithmetic  22.7 us (13%)
  between operations  16 us (9%)
  starting transfers between devices  4.68 us (3%)
    all_gather x1, waiting for transfers between devices, on_device(): lax.all_gather(own_keys, 'token', axis=1, tiled=True)  40.3 us
    all_gather x1, waiting for transfers between devices, on_device(): lax.all_gather(values, 'token', axis=1, tiled=True)  30.9 us
    unnamed x19, local copies, waits for them, and re-layouts  10.7 us
    convert_element_type x1, other arithmetic, on_device(): (later + attn_gate * attended.astype(jnp.float32)).astype(jnp.bfloat16)  10 us
    dot_general x1, matrix products, on_device(): jnp.einsum('b,bfsd->fsd', mix_after, stack, preferred_element_type=jnp.fl...  10 us
    dot_general x1, matrix products, on_device(): jnp.einsum('b,bfsd->fsd', mix_before, stack, preferred_element_type=jnp.f...  8.41 us
    convert_element_type x2, local copies, waits for them, and re-layouts, on_device(): attended.astype(jnp.float32)  6.62 us
    ppermute x2, waiting for transfers between devices, from_behind(): return lax.ppermute(value, axis, pairs)  6.47 us
  transfers between devices with their start and end apart: 4, of which 3 were waited for; matrix products, arithmetic and copies ran while one was open for 12% of the time, Pallas kernels for 0%

commit v1 on v0

v1 whole, which is shorter than its diff:
```python
import functools
import math

import jax
import jax.numpy as jnp
from jax import lax
from jax.experimental import pallas as pl
from jax.experimental.pallas import tpu as pltpu
from jax.sharding import PartitionSpec as P

HEAD_DIM = 128
MAXOV = 4
HEADS_PER_CHUNK = 2
KEYS_AHEAD = 6
VALUES_AHEAD = 4
NORM_COLS = 512
MESH = pl.DeviceIdType.MESH


def kernel(
    peers,
    windows,
    lat_ref,
    q_ref,
    k_ref,
    cached_ref,
    plan_ref,
    refresh_ref,
    gain_ref,
    gate_ref,
    inter_ref,
    out_ref,
    k_all,
    v_all,
    q_own,
    lat_own,
    cached_own,
    later,
    hidden,
    pre,
    from_prev,
    from_next,
    blended,
    load_sem,
    qk_sem,
    k_send,
    k_recv,
    v_send,
    v_recv,
    slab_send,
    slab_recv,
    out_sem,
):
    blocks = cached_ref.shape[0]
    _, frames, spots, width = lat_ref.shape
    rows = frames * spots
    depth = HEAD_DIM
    cols = HEADS_PER_CHUNK * depth
    chunks = width // cols
    scale = math.log2(math.e) / math.sqrt(depth)
    window = lax.axis_index("window")
    token = lax.axis_index("token")
    after = lax.rem(window + 1, windows)
    before = lax.rem(window + windows - 1, windows)

    def span(c):
        return pl.ds(pl.multiple_of(c * cols, cols), cols)

    def latent_load(f):
        return pltpu.make_async_copy(lat_ref.at[0, f], lat_own.at[f], load_sem.at[0, f])

    def cached_load(f):
        return pltpu.make_async_copy(
            cached_ref.at[:, 0, f], cached_own.at[:, f], load_sem.at[1, f]
        )

    def key_load():
        return pltpu.make_async_copy(k_ref.at[0], k_all.at[0], qk_sem.at[0])

    def query_load():
        return pltpu.make_async_copy(q_ref.at[0], q_own, qk_sem.at[1])

    def peer(r):
        return {"token": lax.rem(token + r, peers)}

    def key_copy(c, r):
        return pltpu.make_async_remote_copy(
            src_ref=k_ref.at[0, :, :, span(c)],
            dst_ref=k_all.at[r, :, :, span(c)],
            send_sem=k_send.at[r - 1, c],
            recv_sem=k_recv.at[r - 1, c],
            device_id=peer(r),
            device_id_type=MESH,
        )

    def value_copy(c, r):
        return pltpu.make_async_remote_copy(
            src_ref=v_all.at[0, :, :, span(c)],
            dst_ref=v_all.at[r, :, :, span(c)],
            send_sem=v_send.at[r - 1, c],
            recv_sem=v_recv.at[r - 1, c],
            device_id=peer(r),
            device_id_type=MESH,
        )

    def slab_to_next(c):
        return pltpu.make_async_remote_copy(
            src_ref=pre.at[pl.ds(frames - MAXOV, MAXOV), :, span(c)],
            dst_ref=from_prev.at[:, :, span(c)],
            send_sem=slab_send.at[0, c],
            recv_sem=slab_recv.at[0, c],
            device_id={"window": after},
            device_id_type=MESH,
        )

    def slab_to_prev(c):
        return pltpu.make_async_remote_copy(
            src_ref=pre.at[pl.ds(0, MAXOV), :, span(c)],
            dst_ref=from_next.at[:, :, span(c)],
            send_sem=slab_send.at[1, c],
            recv_sem=slab_recv.at[1, c],
            device_id={"window": before},
            device_id_type=MESH,
        )

    def out_copy(c):
        return pltpu.make_async_copy(
            blended.at[:, :, span(c)], out_ref.at[0, :, :, span(c)], out_sem.at[c]
        )

    barrier = pltpu.get_barrier_semaphore()
    for r in range(1, peers):
        pl.semaphore_signal(barrier, inc=1, device_id=peer(r), device_id_type=MESH)
    pl.semaphore_signal(barrier, inc=1, device_id={"window": after}, device_id_type=MESH)
    pl.semaphore_signal(barrier, inc=1, device_id={"window": before}, device_id_type=MESH)

    for f in range(frames):
        latent_load(f).start()
        cached_load(f).start()
    key_load().start()
    query_load().start()

    pl.semaphore_wait(barrier, peers - 1 + 2)

    def start_keys(c):
        for r in range(1, peers):
            key_copy(c, r).start()

    def start_values(c):
        for r in range(1, peers):
            value_copy(c, r).start()

    keys_ahead = min(KEYS_AHEAD, chunks)
    values_ahead = min(VALUES_AHEAD, chunks)

    @pl.loop(0, keys_ahead)
    def _(c):
        start_keys(c)

    chosen = refresh_ref[window]
    mix_before = []
    mix_after = []
    for b in range(blocks):
        planned = plan_ref[b]
        mix_before.append(jnp.where(b < chosen, planned, 0).astype(jnp.float32))
        mix_after.append(jnp.where(b > chosen, planned, 0).astype(jnp.float32))

    @pl.loop(0, frames)
    def _(f):
        latent_load(f).wait()
        cached_load(f).wait()
        squares = jnp.zeros((spots, NORM_COLS), jnp.float32)
        for start in range(0, width, NORM_COLS):
            part = pl.ds(start, NORM_COLS)
            held = lat_own[f, :, part].astype(jnp.float32)
            rest = jnp.zeros_like(held)
            for b in range(blocks):
                layer = cached_own[b, f, :, part].astype(jnp.float32)
                held = held + mix_before[b] * layer
                rest = rest + mix_after[b] * layer
            squares = squares + held * held
            hidden[:, part] = held
            later[f, :, part] = held + rest
        mean_square = jnp.sum(squares, axis=-1, keepdims=True) * (1.0 / width)
        inv = lax.rsqrt(mean_square + 1e-06)
        for start in range(0, width, NORM_COLS):
            part = pl.ds(start, NORM_COLS)
            v_all[0, f, :, part] = (hidden[:, part] * inv * gain_ref[:, part]).astype(
                jnp.bfloat16
            )

    @pl.loop(0, values_ahead)
    def _(c):
        start_values(c)

    key_load().wait()
    query_load().wait()

    ov_next = inter_ref[window]
    ov_prev = inter_ref[before]
    step_next = 1.0 / jnp.full((1, 128), ov_next + 1, jnp.int32).astype(jnp.float32)
    step_prev = 1.0 / jnp.full((1, 128), ov_prev + 1, jnp.int32).astype(jnp.float32)

    def blend(c):
        slab_to_next(c).wait_recv()
        slab_to_prev(c).wait_recv()
        for h in range(HEADS_PER_CHUNK):
            here = pl.ds(pl.multiple_of(c * cols + h * depth, depth), depth)
            for f in range(frames):
                mine = pre[f, :, here]
                if f < MAXOV:
                    inside = jnp.where(f < ov_prev, 1, 0).astype(jnp.float32)
                    ramp = (f + 1.0) * step_prev
                    partner = jnp.zeros((spots, depth), jnp.float32)
                    for s in range(f, MAXOV):
                        hit = jnp.where(MAXOV - ov_prev + f == s, 1, 0).astype(jnp.float32)
                        partner = partner + hit * from_prev[s, :, here].astype(jnp.float32)
                    own_part = 1.0 - inside * (1.0 - ramp)
                    mixed = own_part * mine.astype(jnp.float32) + (
                        inside * (1.0 - ramp)
                    ) * partner
                    mine = mixed.astype(jnp.bfloat16)
                elif f >= frames - MAXOV:
                    g = f - (frames - MAXOV)
                    place = g - MAXOV + ov_next
                    inside = jnp.where(place >= 0, 1, 0).astype(jnp.float32)
                    ramp = (place + 1).astype(jnp.float32) * step_next
                    partner = jnp.zeros((spots, depth), jnp.float32)
                    for s in range(g + 1):
                        hit = jnp.where(place == s, 1, 0).astype(jnp.float32)
                        partner = partner + hit * from_next[s, :, here].astype(jnp.float32)
                    mixed = (1.0 - inside * ramp) * mine.astype(jnp.float32) + (
                        inside * ramp
                    ) * partner
                    mine = mixed.astype(jnp.bfloat16)
                blended[f, :, here] = mine
        out_copy(c).start()

    @pl.loop(0, chunks)
    def _(c):
        @pl.when(c + keys_ahead < chunks)
        def _():
            start_keys(c + keys_ahead)

        @pl.when(c + values_ahead < chunks)
        def _():
            start_values(c + values_ahead)

        for r in range(1, peers):
            key_copy(c, r).wait_recv()
            value_copy(c, r).wait_recv()
        for h in range(HEADS_PER_CHUNK):
            here = pl.ds(pl.multiple_of(c * cols + h * depth, depth), depth)
            head_q = q_own[:, :, here].reshape(rows, depth)
            head_k = k_all[:, :, :, here].reshape(peers * rows, depth)
            head_v = v_all[:, :, :, here].reshape(peers * rows, depth)
            scores = lax.dot_general(
                head_q, head_k, (((1,), (1,)), ((), ())), preferred_element_type=jnp.float32
            )
            peak = jnp.max(scores, axis=-1, keepdims=True)
            weights = jnp.exp2((scores - peak) * scale)
            summed = jnp.sum(weights, axis=-1, keepdims=True)
            total = jnp.dot(
                weights.astype(jnp.bfloat16), head_v, preferred_element_type=jnp.float32
            )
            attended = (total * (1.0 / summed)).astype(jnp.bfloat16).astype(jnp.float32)
            mixed = later[:, :, here].reshape(rows, depth) + gate_ref[:, here] * attended
            pre[:, :, here] = mixed.astype(jnp.bfloat16).reshape(frames, spots, depth)
        slab_to_next(c).start()
        slab_to_prev(c).start()

        @pl.when(c >= 1)
        def _():
            blend(c - 1)

    blend(chunks - 1)

    @pl.loop(0, chunks)
    def _(c):
        for r in range(1, peers):
            key_copy(c, r).wait_send()
            value_copy(c, r).wait_send()
        slab_to_next(c).wait_send()
        slab_to_prev(c).wait_send()
        out_copy(c).wait()


def on_device(
    peers,
    windows,
    latents,
    queries,
    attn_keys,
    cached,
    plan,
    refresh,
    value_gain,
    attn_gate,
    intersections,
):
    _, frames, spots, width = latents.shape
    blocks = cached.shape[0]
    chunks = width // (HEADS_PER_CHUNK * HEAD_DIM)
    rows = frames * spots
    bf16, f32 = jnp.bfloat16, jnp.float32
    anywhere = pl.BlockSpec(memory_space=pl.ANY)
    scalars = pl.BlockSpec(memory_space=pltpu.SMEM)
    vectors = pl.BlockSpec(memory_space=pltpu.VMEM)
    others = max(peers - 1, 1)
    flops = 4 * rows * rows * peers * width
    return pl.pallas_call(
        functools.partial(kernel, peers, windows),
        out_shape=jax.ShapeDtypeStruct(latents.shape, bf16),
        in_specs=[anywhere] * 4 + [scalars] * 2 + [vectors] * 2 + [scalars],
        out_specs=anywhere,
        scratch_shapes=[
            pltpu.VMEM((peers, frames, spots, width), bf16),
            pltpu.VMEM((peers, frames, spots, width), bf16),
            pltpu.VMEM((frames, spots, width), bf16),
            pltpu.VMEM((frames, spots, width), bf16),
            pltpu.VMEM((blocks, frames, spots, width), bf16),
            pltpu.VMEM((frames, spots, width), f32),
            pltpu.VMEM((spots, width), f32),
            pltpu.VMEM((frames, spots, width), bf16),
            pltpu.VMEM((MAXOV, spots, width), bf16),
            pltpu.VMEM((MAXOV, spots, width), bf16),
            pltpu.VMEM((frames, spots, width), bf16),
            pltpu.SemaphoreType.DMA((2, frames)),
            pltpu.SemaphoreType.DMA((2,)),
            pltpu.SemaphoreType.DMA((others, chunks)),
            pltpu.SemaphoreType.DMA((others, chunks)),
            pltpu.SemaphoreType.DMA((others, chunks)),
            pltpu.SemaphoreType.DMA((others, chunks)),
            pltpu.SemaphoreType.DMA((2, chunks)),
            pltpu.SemaphoreType.DMA((2, chunks)),
            pltpu.SemaphoreType.DMA((chunks,)),
        ],
        compiler_params=pltpu.CompilerParams(
            collective_id=0, has_side_effects=True, vmem_limit_bytes=58 * 1024 * 1024
        ),
        cost_estimate=pl.CostEstimate(
            flops=flops,
            bytes_accessed=2 * rows * width * (4 + blocks),
            transcendentals=rows * rows * peers * (width // HEAD_DIM),
        ),
    )(
        latents,
        queries,
        attn_keys,
        cached,
        plan,
        refresh,
        value_gain.reshape(1, width),
        attn_gate.reshape(1, width),
        intersections,
    )


def solution(mesh):
    in_specs = (
        P("window", None, "token", None),
        P("window", None, "token", None),
        P("window", None, "token", None),
        P(None, "window", None, "token", None),
        P(),
        P(),
        P(),
        P(),
        P(),
    )
    out_specs = P("window", None, "token", None)
    return jax.shard_map(
        functools.partial(on_device, mesh.shape["token"], mesh.shape["window"]),
        mesh=mesh,
        in_specs=in_specs,
        out_specs=out_specs,
        check_vma=False,
    )
```

time: 179 us -> 82.6 us (0.46); the launches traced: 176 us -> 82.4 us
  Pallas kernels: 0 us -> 79.8 us
  waiting for transfers between devices: 78.4 us -> 0 us
  matrix products: 31.4 us -> 0 us
  other arithmetic: 22.7 us -> 0 us
  local copies, waits for them, and re-layouts: 22.9 us -> 2.58 us
  between operations: 16 us -> 0.01 us
  starting transfers between devices: 4.68 us -> 0 us
    pallas_call x0 -> x1, Pallas kernels: none -> 79.8 us  [on_device(): pl.pallas_call(functools.partial(kernel, peers, windows), out_shape=jax.S...]
    all_gather x2 -> x0, waiting for transfers between devices: 71.2 us -> none  [the longest x1 40.3 us: on_device(): lax.all_gather(own_keys, 'token', axis=1, tiled=True)]
    dot_general x6 -> x0, matrix products: 31.4 us -> none  [the longest x1 10 us: on_device(): jnp.einsum('b,bfsd->fsd', mix_after, stack, preferred_element_type=jnp.fl...]
    convert_element_type x2 -> x0, other arithmetic: 12.7 us -> none  [the longest x1 10 us: on_device(): (later + attn_gate * attended.astype(jnp.float32)).astype(jnp.bfloat16)]
    reduce_sum x3 -> x0, other arithmetic: 9.21 us -> none  [the longest x1 4.7 us: on_device(): mean_square = jnp.mean(hidden * hidden, axis=-1, keepdims=True)]
    convert_element_type x3 -> x0, local copies, waits for them, and re-layouts: 8.86 us -> none  [the longest x2 6.62 us: on_device(): attended.astype(jnp.float32)]
    unnamed x19 -> x1, local copies, waits for them, and re-layouts: 10.7 us -> 2.58 us
    ppermute x2 -> x0, waiting for transfers between devices: 6.47 us -> none  [from_behind(): return lax.ppermute(value, axis, pairs)]
  transfers between devices with their start and end apart: 4 -> 0, of which waited for: 3 -> 0; matrix products, arithmetic and copies ran while one was open for 12% -> 0% of each run, Pallas kernels for 0% -> 0%
where the time goes in v1:
time: 82.6 us; the launch traced here: 82.4 us
  Pallas kernels  79.8 us (97%)
  local copies, waits for them, and re-layouts  2.58 us (3%)
    pallas_call x1, Pallas kernels, on_device(): pl.pallas_call(functools.partial(kernel, peers, windows), out_shape=jax.S...  79.8 us
    unnamed x1, local copies, waits for them, and re-layouts  2.58 us

profile of v1, /device:TPU:0, one launch (start us, length us, event | category | flops | bytes accessed | tf_op | source)
XLA Modules:
  0.0 82.4 jit_solution(1257640472911791550)
XLA Ops:
  0.0 79.8 %shard_map.91 = bf16[1,9,16,5120]{3,2,1,0:T(8,128)(2,1)} custom-call(bf16[1,9,16,5120]{3,2,1,0:T(8,128)(2,1)} %lat_ref.1, bf16[1,9,16,5120]{3,2,1,0:T(8,128)(2,1)} %q_ref.1, bf16[1,9,16,5120]{3,2,1,0:T(8,128)(2,1)} %k_ref.1, bf16[4,1,9,16,5120]{4,3,2,1,0:T(8,128)(2,1)} %cached_ref.1, s32[4]{0:T(128)} %plan_ref.1, s32[16]{0:T(128)} %refresh_ref.1, ...), custom_call_target="tpu_custom_call" | custom-call | flops 849346560 | bytes 11796480 | tf_op jit(solution)/shard_map/pallas_call | solution.py:311
  79.8 2.6 %copy.11 = bf16[1,9,16,5120]{3,2,1,0:T(8,128)(2,1)} copy(bf16[1,9,16,5120]{3,2,1,0:T(8,128)(2,1)} %shard_map.91) | data formatting | bytes 2949120

commit v2 on v1

v2 whole, which is shorter than its diff:
```python
import functools
import math

import jax
import jax.numpy as jnp
from jax import lax
from jax.experimental import pallas as pl
from jax.experimental.pallas import tpu as pltpu
from jax.sharding import PartitionSpec as P

HEAD_DIM = 128
MAXOV = 4
KEYS_AHEAD = 14
VALUES_AHEAD = 8
NORM_COLS = 512
MESH = pl.DeviceIdType.MESH


def kernel(
    peers,
    windows,
    lat_ref,
    q_ref,
    k_ref,
    cached_ref,
    plan_ref,
    refresh_ref,
    gain_ref,
    gate_ref,
    inter_ref,
    out_ref,
    k_all,
    v_all,
    q_own,
    lat_own,
    cached_own,
    later,
    hidden,
    pre,
    from_prev,
    from_next,
    probs,
    sums,
    load_sem,
    key_sem,
    query_sem,
    k_send,
    k_recv,
    v_send,
    v_recv,
    slab_send,
    slab_recv,
):
    blocks = cached_ref.shape[0]
    _, frames, spots, width = lat_ref.shape
    rows = frames * spots
    depth = HEAD_DIM
    heads = width // depth
    scale = math.log2(math.e) / math.sqrt(depth)
    window = lax.axis_index("window")
    token = lax.axis_index("token")
    after = lax.rem(window + 1, windows)
    before = lax.rem(window + windows - 1, windows)

    def span(h):
        return pl.ds(pl.multiple_of(h * depth, depth), depth)

    def latent_load(f):
        return pltpu.make_async_copy(lat_ref.at[0, f], lat_own.at[f], load_sem.at[0, f])

    def cached_load(f):
        return pltpu.make_async_copy(
            cached_ref.at[:, 0, f], cached_own.at[:, f], load_sem.at[1, f]
        )

    def key_load(h):
        return pltpu.make_async_copy(
            k_ref.at[0, :, :, span(h)], k_all.at[0, h], key_sem.at[h]
        )

    def query_load():
        return pltpu.make_async_copy(q_ref.at[0], q_own, query_sem.at[0])

    def peer(r):
        return {"token": lax.rem(token + r, peers)}

    def key_copy(h, r):
        return pltpu.make_async_remote_copy(
            src_ref=k_all.at[0, h],
            dst_ref=k_all.at[r, h],
            send_sem=k_send.at[r - 1, h],
            recv_sem=k_recv.at[r - 1, h],
            device_id=peer(r),
            device_id_type=MESH,
        )

    def value_copy(h, r):
        return pltpu.make_async_remote_copy(
            src_ref=v_all.at[0, h],
            dst_ref=v_all.at[r, h],
            send_sem=v_send.at[r - 1, h],
            recv_sem=v_recv.at[r - 1, h],
            device_id=peer(r),
            device_id_type=MESH,
        )

    def slab_to_next(h):
        return pltpu.make_async_remote_copy(
            src_ref=pre.at[h, pl.ds(frames - MAXOV, MAXOV)],
            dst_ref=from_prev.at[h],
            send_sem=slab_send.at[0, h],
            recv_sem=slab_recv.at[0, h],
            device_id={"window": after},
            device_id_type=MESH,
        )

    def slab_to_prev(h):
        return pltpu.make_async_remote_copy(
            src_ref=pre.at[h, pl.ds(0, MAXOV)],
            dst_ref=from_next.at[h],
            send_sem=slab_send.at[1, h],
            recv_sem=slab_recv.at[1, h],
            device_id={"window": before},
            device_id_type=MESH,
        )

    barrier = pltpu.get_barrier_semaphore()
    for r in range(1, peers):
        pl.semaphore_signal(barrier, inc=1, device_id=peer(r), device_id_type=MESH)
    pl.semaphore_signal(barrier, inc=1, device_id={"window": after}, device_id_type=MESH)
    pl.semaphore_signal(barrier, inc=1, device_id={"window": before}, device_id_type=MESH)

    keys_ahead = min(KEYS_AHEAD, heads)
    values_ahead = min(VALUES_AHEAD, heads)

    @pl.loop(0, keys_ahead)
    def _(h):
        key_load(h).start()

    for f in range(frames):
        latent_load(f).start()
        cached_load(f).start()

    @pl.loop(keys_ahead, heads)
    def _(h):
        key_load(h).start()

    query_load().start()

    pl.semaphore_wait(barrier, peers - 1 + 2)

    def start_keys(h):
        key_load(h).wait()
        for r in range(1, peers):
            key_copy(h, r).start()

    def start_values(h):
        for r in range(1, peers):
            value_copy(h, r).start()

    @pl.loop(0, keys_ahead)
    def _(h):
        start_keys(h)

    chosen = refresh_ref[window]
    mix_before = []
    mix_after = []
    for b in range(blocks):
        planned = plan_ref[b]
        mix_before.append(jnp.where(b < chosen, planned, 0).astype(jnp.float32))
        mix_after.append(jnp.where(b > chosen, planned, 0).astype(jnp.float32))

    @pl.loop(0, frames)
    def _(f):
        latent_load(f).wait()
        cached_load(f).wait()
        squares = jnp.zeros((spots, NORM_COLS), jnp.float32)
        for start in range(0, width, NORM_COLS):
            part = pl.ds(start, NORM_COLS)
            held = lat_own[f, :, part].astype(jnp.float32)
            rest = jnp.zeros_like(held)
            for b in range(blocks):
                layer = cached_own[b, f, :, part].astype(jnp.float32)
                held = held + mix_before[b] * layer
                rest = rest + mix_after[b] * layer
            squares = squares + held * held
            hidden[:, part] = held
            later[f, :, part] = held + rest
        mean_square = jnp.sum(squares, axis=-1, keepdims=True) * (1.0 / width)
        inv = lax.rsqrt(mean_square + 1e-06)
        for h in range(heads):
            part = pl.ds(h * depth, depth)
            v_all[0, h, f] = (hidden[:, part] * inv * gain_ref[:, part]).astype(jnp.bfloat16)

    @pl.loop(0, values_ahead)
    def _(h):
        start_values(h)

    query_load().wait()

    ov_next = inter_ref[window]
    ov_prev = inter_ref[before]
    step_next = 1.0 / jnp.full((1, depth), ov_next + 1, jnp.int32).astype(jnp.float32)
    step_prev = 1.0 / jnp.full((1, depth), ov_prev + 1, jnp.int32).astype(jnp.float32)

    def blend(h):
        slab_to_next(h).wait_recv()
        slab_to_prev(h).wait_recv()
        here = span(h)
        for f in range(frames):
            mine = pre[h, f]
            if f < MAXOV:
                inside = jnp.where(f < ov_prev, 1, 0).astype(jnp.float32)
                ramp = (f + 1.0) * step_prev
                partner = jnp.zeros((spots, depth), jnp.float32)
                for s in range(f, MAXOV):
                    hit = jnp.where(MAXOV - ov_prev + f == s, 1, 0).astype(jnp.float32)
                    partner = partner + hit * from_prev[h, s].astype(jnp.float32)
                share = inside * (1.0 - ramp)
                mixed = (1.0 - share) * mine.astype(jnp.float32) + share * partner
                mine = mixed.astype(jnp.bfloat16)
            elif f >= frames - MAXOV:
                g = f - (frames - MAXOV)
                place = g - MAXOV + ov_next
                inside = jnp.where(place >= 0, 1, 0).astype(jnp.float32)
                ramp = (place + 1).astype(jnp.float32) * step_next
                partner = jnp.zeros((spots, depth), jnp.float32)
                for s in range(g + 1):
                    hit = jnp.where(place == s, 1, 0).astype(jnp.float32)
                    partner = partner + hit * from_next[h, s].astype(jnp.float32)
                share = inside * ramp
                mixed = (1.0 - share) * mine.astype(jnp.float32) + share * partner
                mine = mixed.astype(jnp.bfloat16)
            out_ref[0, f, :, here] = mine

    def weigh(h):
        for r in range(1, peers):
            key_copy(h, r).wait_recv()
        head_q = q_own[:, :, span(h)].reshape(rows, depth)
        head_k = k_all[:, h].reshape(peers * rows, depth)
        scores = lax.dot_general(
            head_q, head_k, (((1,), (1,)), ((), ())), preferred_element_type=jnp.float32
        )
        peak = jnp.max(scores, axis=-1, keepdims=True)
        weights = jnp.exp2((scores - peak) * scale)
        summed = jnp.sum(weights, axis=-1, keepdims=True)
        slot = lax.rem(h, 2)
        probs[slot] = weights.astype(jnp.bfloat16)
        sums[slot] = jnp.broadcast_to(1.0 / summed, (rows, depth))

    def attend(h):
        for r in range(1, peers):
            value_copy(h, r).wait_recv()
        slot = lax.rem(h, 2)
        head_v = v_all[:, h].reshape(peers * rows, depth)
        total = jnp.dot(probs[slot], head_v, preferred_element_type=jnp.float32)
        attended = (total * sums[slot]).astype(jnp.bfloat16).astype(jnp.float32)
        mixed = later[:, :, span(h)].reshape(rows, depth) + gate_ref[:, span(h)] * attended
        pre[h] = mixed.astype(jnp.bfloat16).reshape(frames, spots, depth)
        slab_to_next(h).start()
        slab_to_prev(h).start()

    weigh(0)

    @pl.loop(0, heads)
    def _(h):
        @pl.when(h + keys_ahead < heads)
        def _():
            start_keys(h + keys_ahead)

        @pl.when(h + values_ahead < heads)
        def _():
            start_values(h + values_ahead)

        attend(h)

        @pl.when(h + 1 < heads)
        def _():
            weigh(h + 1)

        @pl.when(h >= 2)
        def _():
            blend(h - 2)

    blend(heads - 2)

    @pl.loop(0, heads)
    def _(h):
        for r in range(1, peers):
            key_copy(h, r).wait_send()
            value_copy(h, r).wait_send()
        slab_to_next(h).wait_send()
        slab_to_prev(h).wait_send()

    blend(heads - 1)


def on_device(
    peers,
    windows,
    latents,
    queries,
    attn_keys,
    cached,
    plan,
    refresh,
    value_gain,
    attn_gate,
    intersections,
):
    _, frames, spots, width = latents.shape
    blocks = cached.shape[0]
    depth = HEAD_DIM
    heads = width // depth
    rows = frames * spots
    bf16, f32 = jnp.bfloat16, jnp.float32
    anywhere = pl.BlockSpec(memory_space=pl.ANY)
    scalars = pl.BlockSpec(memory_space=pltpu.SMEM)
    vectors = pl.BlockSpec(memory_space=pltpu.VMEM)
    others = max(peers - 1, 1)
    flops = 4 * rows * rows * peers * width
    return pl.pallas_call(
        functools.partial(kernel, peers, windows),
        out_shape=pltpu.VMEM(latents.shape, bf16),
        in_specs=[anywhere] * 4 + [scalars] * 2 + [vectors] * 2 + [scalars],
        out_specs=vectors,
        scratch_shapes=[
            pltpu.VMEM((peers, heads, frames, spots, depth), bf16),
            pltpu.VMEM((peers, heads, frames, spots, depth), bf16),
            pltpu.VMEM((frames, spots, width), bf16),
            pltpu.VMEM((frames, spots, width), bf16),
            pltpu.VMEM((blocks, frames, spots, width), bf16),
            pltpu.VMEM((frames, spots, width), f32),
            pltpu.VMEM((spots, width), f32),
            pltpu.VMEM((heads, frames, spots, depth), bf16),
            pltpu.VMEM((heads, MAXOV, spots, depth), bf16),
            pltpu.VMEM((heads, MAXOV, spots, depth), bf16),
            pltpu.VMEM((2, rows, peers * rows), bf16),
            pltpu.VMEM((2, rows, depth), f32),
            pltpu.SemaphoreType.DMA((2, frames)),
            pltpu.SemaphoreType.DMA((heads,)),
            pltpu.SemaphoreType.DMA((1,)),
            pltpu.SemaphoreType.DMA((others, heads)),
            pltpu.SemaphoreType.DMA((others, heads)),
            pltpu.SemaphoreType.DMA((others, heads)),
            pltpu.SemaphoreType.DMA((others, heads)),
            pltpu.SemaphoreType.DMA((2, heads)),
            pltpu.SemaphoreType.DMA((2, heads)),
        ],
        compiler_params=pltpu.CompilerParams(
            collective_id=0, has_side_effects=True, vmem_limit_bytes=56 * 1024 * 1024
        ),
        cost_estimate=pl.CostEstimate(
            flops=flops,
            bytes_accessed=2 * rows * width * (4 + blocks),
            transcendentals=rows * rows * peers * heads,
        ),
    )(
        latents,
        queries,
        attn_keys,
        cached,
        plan,
        refresh,
        value_gain.reshape(1, width),
        attn_gate.reshape(1, width),
        intersections,
    )


def solution(mesh):
    in_specs = (
        P("window", None, "token", None),
        P("window", None, "token", None),
        P("window", None, "token", None),
        P(None, "window", None, "token", None),
        P(),
        P(),
        P(),
        P(),
        P(),
    )
    out_specs = P("window", None, "token", None)
    return jax.shard_map(
        functools.partial(on_device, mesh.shape["token"], mesh.shape["window"]),
        mesh=mesh,
        in_specs=in_specs,
        out_specs=out_specs,
        check_vma=False,
    )
```

time: 82.6 us -> 83.3 us (level)
  Pallas kernels: 79.8 us -> 82 us
  local copies, waits for them, and re-layouts: 2.58 us -> 1.11 us
    pallas_call x1, Pallas kernels: 79.8 us -> 82 us  [on_device(): pl.pallas_call(functools.partial(kernel, peers, windows), out_shape=pltpu...]
    unnamed x1, local copies, waits for them, and re-layouts: 2.58 us -> 1.11 us
where the time goes in v2:
time: 83.3 us; the launch traced here: 83.1 us
  Pallas kernels  82 us (98%)
  local copies, waits for them, and re-layouts  1.11 us (1%)
    pallas_call x1, Pallas kernels, on_device(): pl.pallas_call(functools.partial(kernel, peers, windows), out_shape=pltpu...  82 us

profile of v2, /device:TPU:0, one launch (start us, length us, event | category | flops | bytes accessed | tf_op | source)
XLA Modules:
  0.0 83.1 jit_solution(17766416357932636433)
XLA Ops:
  0.0 82.0 %shard_map.91 = bf16[1,9,16,5120]{3,2,1,0:T(8,128)(2,1)S(1)} custom-call(bf16[1,9,16,5120]{3,2,1,0:T(8,128)(2,1)} %lat_ref.1, bf16[1,9,16,5120]{3,2,1,0:T(8,128)(2,1)} %q_ref.1, bf16[1,9,16,5120]{3,2,1,0:T(8,128)(2,1)} %k_ref.1, bf16[4,1,9,16,5120]{4,3,2,1,0:T(8,128)(2,1)} %cached_ref.1, s32[4]{0:T(128)} %plan_ref.1, s32[16]{0:T(128)} %refresh_ref.1, ...), custom_call_target="tpu_custom_call" | custom-call | flops 849346560 | bytes 11796480 | tf_op jit(solution)/shard_map/pallas_call | solution.py:322
  82.0 1.1 %copy.11 = bf16[1,9,16,5120]{3,2,1,0:T(8,128)(2,1)} copy(bf16[1,9,16,5120]{3,2,1,0:T(8,128)(2,1)S(1)} %shard_map.91) | data formatting | bytes 2949120

commit v3 on v1

v3 whole, which is shorter than its diff:
```python
import functools
import math

import jax
import jax.numpy as jnp
from jax import lax
from jax.experimental import pallas as pl
from jax.experimental.pallas import tpu as pltpu
from jax.sharding import PartitionSpec as P

HEAD_DIM = 128
MAXOV = 4
HEADS_PER_CHUNK = 2
KEYS_FIRST = 8
KEYS_AHEAD = 5
VALUES_AHEAD = 4
NORM_COLS = 512
MESH = pl.DeviceIdType.MESH


def kernel(
    peers,
    windows,
    lat_ref,
    q_ref,
    k_ref,
    cached_ref,
    plan_ref,
    refresh_ref,
    gain_ref,
    gate_ref,
    inter_ref,
    out_ref,
    k_all,
    v_all,
    q_own,
    lat_own,
    cached_own,
    later,
    hidden,
    pre,
    from_prev,
    from_next,
    probs,
    sums,
    gain,
    gate,
    plan,
    refresh,
    inter,
    load_sem,
    key_sem,
    small_sem,
    k_send,
    k_recv,
    v_send,
    v_recv,
    slab_send,
    slab_recv,
):
    blocks = cached_ref.shape[0]
    _, frames, spots, width = lat_ref.shape
    rows = frames * spots
    depth = HEAD_DIM
    cols = HEADS_PER_CHUNK * depth
    chunks = width // cols
    scale = math.log2(math.e) / math.sqrt(depth)
    window = lax.axis_index("window")
    token = lax.axis_index("token")
    after = lax.rem(window + 1, windows)
    before = lax.rem(window + windows - 1, windows)

    def span(c):
        return pl.ds(pl.multiple_of(c * cols, cols), cols)

    def head_span(c, i):
        return pl.ds(pl.multiple_of(c * cols + i * depth, depth), depth)

    def latent_load(f):
        return pltpu.make_async_copy(lat_ref.at[0, f], lat_own.at[f], load_sem.at[0, f])

    def cached_load(f):
        return pltpu.make_async_copy(
            cached_ref.at[:, 0, f], cached_own.at[:, f], load_sem.at[1, f]
        )

    def key_load(c):
        return pltpu.make_async_copy(
            k_ref.at[0, :, :, span(c)], k_all.at[0, c], key_sem.at[c]
        )

    def query_load():
        return pltpu.make_async_copy(q_ref.at[0], q_own, small_sem.at[0])

    small_loads = [
        pltpu.make_async_copy(source, held, small_sem.at[i + 1])
        for i, (source, held) in enumerate(
            (
                (plan_ref, plan),
                (refresh_ref, refresh),
                (gain_ref, gain),
                (gate_ref, gate),
                (inter_ref, inter),
            )
        )
    ]

    def peer(r):
        return {"token": lax.rem(token + r, peers)}

    def key_copy(c, r):
        return pltpu.make_async_remote_copy(
            src_ref=k_ref.at[0, :, :, span(c)],
            dst_ref=k_all.at[r, c],
            send_sem=k_send.at[r - 1, c],
            recv_sem=k_recv.at[r - 1, c],
            device_id=peer(r),
            device_id_type=MESH,
        )

    def value_copy(c, r):
        return pltpu.make_async_remote_copy(
            src_ref=v_all.at[0, c],
            dst_ref=v_all.at[r, c],
            send_sem=v_send.at[r - 1, c],
            recv_sem=v_recv.at[r - 1, c],
            device_id=peer(r),
            device_id_type=MESH,
        )

    def slab_to_next(c):
        return pltpu.make_async_remote_copy(
            src_ref=pre.at[c, pl.ds(frames - MAXOV, MAXOV)],
            dst_ref=from_prev.at[c],
            send_sem=slab_send.at[0, c],
            recv_sem=slab_recv.at[0, c],
            device_id={"window": after},
            device_id_type=MESH,
        )

    def slab_to_prev(c):
        return pltpu.make_async_remote_copy(
            src_ref=pre.at[c, pl.ds(0, MAXOV)],
            dst_ref=from_next.at[c],
            send_sem=slab_send.at[1, c],
            recv_sem=slab_recv.at[1, c],
            device_id={"window": before},
            device_id_type=MESH,
        )

    barrier = pltpu.get_barrier_semaphore()
    for r in range(1, peers):
        pl.semaphore_signal(barrier, inc=1, device_id=peer(r), device_id_type=MESH)
    pl.semaphore_signal(barrier, inc=1, device_id={"window": after}, device_id_type=MESH)
    pl.semaphore_signal(barrier, inc=1, device_id={"window": before}, device_id_type=MESH)

    pl.semaphore_wait(barrier, peers - 1 + 2)

    keys_first = min(KEYS_FIRST, chunks)
    values_ahead = min(VALUES_AHEAD, chunks)

    def start_keys(c):
        for r in range(1, peers):
            key_copy(c, r).start()

    def start_values(c):
        for r in range(1, peers):
            value_copy(c, r).start()

    @pl.loop(0, keys_first)
    def _(c):
        start_keys(c)

    for load in small_loads:
        load.start()

    @pl.loop(0, frames)
    def _(f):
        latent_load(f).start()
        cached_load(f).start()

    query_load().start()

    @pl.loop(0, chunks)
    def _(c):
        key_load(c).start()

    for load in small_loads:
        load.wait()

    chosen = refresh[window]
    mix_before = []
    mix_after = []
    for b in range(blocks):
        planned = plan[b]
        mix_before.append(jnp.where(b < chosen, planned, 0).astype(jnp.float32))
        mix_after.append(jnp.where(b > chosen, planned, 0).astype(jnp.float32))

    @pl.loop(0, frames)
    def _(f):
        latent_load(f).wait()
        cached_load(f).wait()
        squares = jnp.zeros((spots, NORM_COLS), jnp.float32)
        for start in range(0, width, NORM_COLS):
            part = pl.ds(start, NORM_COLS)
            held = lat_own[f, :, part].astype(jnp.float32)
            rest = jnp.zeros_like(held)
            for b in range(blocks):
                layer = cached_own[b, f, :, part].astype(jnp.float32)
                held = held + mix_before[b] * layer
                rest = rest + mix_after[b] * layer
            squares = squares + held * held
            hidden[:, part] = held
            later[f, :, part] = held + rest
        mean_square = jnp.sum(squares, axis=-1, keepdims=True) * (1.0 / width)
        inv = lax.rsqrt(mean_square + 1e-06)
        for c in range(chunks):
            part = pl.ds(c * cols, cols)
            v_all[0, c, f] = (hidden[:, part] * inv * gain[:, part]).astype(jnp.bfloat16)

    @pl.loop(0, values_ahead)
    def _(c):
        start_values(c)

    query_load().wait()

    ov_next = inter[window]
    ov_prev = inter[before]
    step_next = 1.0 / jnp.full((1, cols), ov_next + 1, jnp.int32).astype(jnp.float32)
    step_prev = 1.0 / jnp.full((1, cols), ov_prev + 1, jnp.int32).astype(jnp.float32)

    def blend(c):
        slab_to_next(c).wait_recv()
        slab_to_prev(c).wait_recv()
        for f in range(frames):
            mine = pre[c, f]
            if f < MAXOV:
                inside = jnp.where(f < ov_prev, 1, 0).astype(jnp.float32)
                ramp = (f + 1.0) * step_prev
                partner = jnp.zeros((spots, cols), jnp.float32)
                for s in range(f, MAXOV):
                    hit = jnp.where(MAXOV - ov_prev + f == s, 1, 0).astype(jnp.float32)
                    partner = partner + hit * from_prev[c, s].astype(jnp.float32)
                share = inside * (1.0 - ramp)
                mixed = (1.0 - share) * mine.astype(jnp.float32) + share * partner
                mine = mixed.astype(jnp.bfloat16)
            elif f >= frames - MAXOV:
                g = f - (frames - MAXOV)
                place = g - MAXOV + ov_next
                inside = jnp.where(place >= 0, 1, 0).astype(jnp.float32)
                ramp = (place + 1).astype(jnp.float32) * step_next
                partner = jnp.zeros((spots, cols), jnp.float32)
                for s in range(g + 1):
                    hit = jnp.where(place == s, 1, 0).astype(jnp.float32)
                    partner = partner + hit * from_next[c, s].astype(jnp.float32)
                share = inside * ramp
                mixed = (1.0 - share) * mine.astype(jnp.float32) + share * partner
                mine = mixed.astype(jnp.bfloat16)
            out_ref[0, f, :, span(c)] = mine

    def weigh(c):
        key_load(c).wait()
        for r in range(1, peers):
            key_copy(c, r).wait_recv()
        slot = lax.rem(c, 2)
        for i in range(HEADS_PER_CHUNK):
            lanes = pl.ds(i * depth, depth)
            head_q = q_own[:, :, head_span(c, i)].reshape(rows, depth)
            head_k = k_all[:, c, :, :, lanes].reshape(peers * rows, depth)
            scores = lax.dot_general(
                head_q, head_k, (((1,), (1,)), ((), ())), preferred_element_type=jnp.float32
            )
            peak = jnp.max(scores, axis=-1, keepdims=True)
            weights = jnp.exp2((scores - peak) * scale)
            summed = jnp.sum(weights, axis=-1, keepdims=True)
            probs[slot, i] = weights.astype(jnp.bfloat16)
            sums[slot, i] = jnp.broadcast_to(1.0 / summed, (rows, depth))

    def attend(c):
        for r in range(1, peers):
            value_copy(c, r).wait_recv()
        slot = lax.rem(c, 2)
        for i in range(HEADS_PER_CHUNK):
            lanes = pl.ds(i * depth, depth)
            here = head_span(c, i)
            head_v = v_all[:, c, :, :, lanes].reshape(peers * rows, depth)
            total = jnp.dot(probs[slot, i], head_v, preferred_element_type=jnp.float32)
            attended = (total * sums[slot, i]).astype(jnp.bfloat16).astype(jnp.float32)
            mixed = later[:, :, here].reshape(rows, depth) + gate[:, here] * attended
            pre[c, :, :, lanes] = mixed.astype(jnp.bfloat16).reshape(frames, spots, depth)
        slab_to_next(c).start()
        slab_to_prev(c).start()

    weigh(0)

    @pl.loop(0, chunks)
    def _(c):
        @pl.when(c + values_ahead < chunks)
        def _():
            start_values(c + values_ahead)

        @pl.when(jnp.logical_and(c + KEYS_AHEAD >= keys_first, c + KEYS_AHEAD < chunks))
        def _():
            start_keys(c + KEYS_AHEAD)

        attend(c)

        @pl.when(c + 1 < chunks)
        def _():
            weigh(c + 1)

        @pl.when(c >= 1)
        def _():
            blend(c - 1)

    @pl.loop(0, chunks)
    def _(c):
        for r in range(1, peers):
            key_copy(c, r).wait_send()
            value_copy(c, r).wait_send()
        slab_to_next(c).wait_send()
        slab_to_prev(c).wait_send()

    blend(chunks - 1)


def on_device(
    peers,
    windows,
    latents,
    queries,
    attn_keys,
    cached,
    plan,
    refresh,
    value_gain,
    attn_gate,
    intersections,
):
    _, frames, spots, width = latents.shape
    blocks = cached.shape[0]
    depth = HEAD_DIM
    heads = width // depth
    chunks = heads // HEADS_PER_CHUNK
    cols = HEADS_PER_CHUNK * depth
    rows = frames * spots
    bf16, f32 = jnp.bfloat16, jnp.float32
    in_hbm = pl.BlockSpec(memory_space=pltpu.HBM)
    vectors = pl.BlockSpec(memory_space=pltpu.VMEM)
    others = max(peers - 1, 1)
    flops = 4 * rows * rows * peers * width
    return pl.pallas_call(
        functools.partial(kernel, peers, windows),
        out_shape=pltpu.VMEM(latents.shape, bf16),
        in_specs=[in_hbm] * 9,
        out_specs=vectors,
        scratch_shapes=[
            pltpu.VMEM((peers, chunks, frames, spots, cols), bf16),
            pltpu.VMEM((peers, chunks, frames, spots, cols), bf16),
            pltpu.VMEM((frames, spots, width), bf16),
            pltpu.VMEM((frames, spots, width), bf16),
            pltpu.VMEM((blocks, frames, spots, width), bf16),
            pltpu.VMEM((frames, spots, width), f32),
            pltpu.VMEM((spots, width), f32),
            pltpu.VMEM((chunks, frames, spots, cols), bf16),
            pltpu.VMEM((chunks, MAXOV, spots, cols), bf16),
            pltpu.VMEM((chunks, MAXOV, spots, cols), bf16),
            pltpu.VMEM((2, HEADS_PER_CHUNK, rows, peers * rows), bf16),
            pltpu.VMEM((2, HEADS_PER_CHUNK, rows, depth), f32),
            pltpu.VMEM((1, width), f32),
            pltpu.VMEM((1, width), f32),
            pltpu.SMEM(plan.shape, jnp.int32),
            pltpu.SMEM(refresh.shape, jnp.int32),
            pltpu.SMEM(intersections.shape, jnp.int32),
            pltpu.SemaphoreType.DMA((2, frames)),
            pltpu.SemaphoreType.DMA((chunks,)),
            pltpu.SemaphoreType.DMA((6,)),
            pltpu.SemaphoreType.DMA((others, chunks)),
            pltpu.SemaphoreType.DMA((others, chunks)),
            pltpu.SemaphoreType.DMA((others, chunks)),
            pltpu.SemaphoreType.DMA((others, chunks)),
            pltpu.SemaphoreType.DMA((2, chunks)),
            pltpu.SemaphoreType.DMA((2, chunks)),
        ],
        compiler_params=pltpu.CompilerParams(
            collective_id=0, has_side_effects=True, vmem_limit_bytes=56 * 1024 * 1024
        ),
        cost_estimate=pl.CostEstimate(
            flops=flops,
            bytes_accessed=2 * rows * width * (4 + blocks),
            transcendentals=rows * rows * peers * heads,
        ),
    )(
        latents,
        queries,
        attn_keys,
        cached,
        plan,
        refresh,
        value_gain.reshape(1, width),
        attn_gate.reshape(1, width),
        intersections,
    )


def solution(mesh):
    in_specs = (
        P("window", None, "token", None),
        P("window", None, "token", None),
        P("window", None, "token", None),
        P(None, "window", None, "token", None),
        P(),
        P(),
        P(),
        P(),
        P(),
    )
    out_specs = P("window", None, "token", None)
    return jax.shard_map(
        functools.partial(on_device, mesh.shape["token"], mesh.shape["window"]),
        mesh=mesh,
        in_specs=in_specs,
        out_specs=out_specs,
        check_vma=False,
    )
```

time: 82.6 us -> 76.8 us (0.930)
  Pallas kernels: 79.8 us -> 75.6 us
  local copies, waits for them, and re-layouts: 2.58 us -> 1.11 us
    pallas_call x1, Pallas kernels: 79.8 us -> 75.6 us  [on_device(): pl.pallas_call(functools.partial(kernel, peers, windows), out_shape=pltpu...]
    unnamed x1, local copies, waits for them, and re-layouts: 2.58 us -> 1.11 us
where the time goes in v3:
time: 76.8 us; the launch traced here: 76.7 us
  Pallas kernels  75.6 us (98%)
  local copies, waits for them, and re-layouts  1.11 us (1%)
    pallas_call x1, Pallas kernels, on_device(): pl.pallas_call(functools.partial(kernel, peers, windows), out_shape=pltpu...  75.6 us

profile of v3, /device:TPU:0, one launch (start us, length us, event | category | flops | bytes accessed | tf_op | source)
XLA Modules:
  0.0 76.7 jit_solution(4351723632685443592)
XLA Ops:
  0.0 75.6 %shard_map.91 = bf16[1,9,16,5120]{3,2,1,0:T(8,128)(2,1)S(1)} custom-call(bf16[1,9,16,5120]{3,2,1,0:T(8,128)(2,1)} %lat_ref.1, bf16[1,9,16,5120]{3,2,1,0:T(8,128)(2,1)} %q_ref.1, bf16[1,9,16,5120]{3,2,1,0:T(8,128)(2,1)} %k_ref.1, bf16[4,1,9,16,5120]{4,3,2,1,0:T(8,128)(2,1)} %cached_ref.1, s32[4]{0:T(128)} %plan_ref.1, s32[16]{0:T(128)} %refresh_ref.1, ...), custom_call_target="tpu_custom_call" | custom-call | flops 849346560 | bytes 11796480 | tf_op jit(solution)/shard_map/pallas_call | solution.py:352
  75.6 1.1 %copy.11 = bf16[1,9,16,5120]{3,2,1,0:T(8,128)(2,1)} copy(bf16[1,9,16,5120]{3,2,1,0:T(8,128)(2,1)S(1)} %shard_map.91) | data formatting | bytes 2949120

commit v4 on v3

--- a/solution.py
+++ b/solution.py
@@ -11,7 +11,7 @@
 HEAD_DIM = 128
 MAXOV = 4
 HEADS_PER_CHUNK = 2
-KEYS_FIRST = 8
+KEYS_FIRST = 12
 KEYS_AHEAD = 5
 VALUES_AHEAD = 4
 NORM_COLS = 512
@@ -118,32 +118,32 @@
             device_id_type=MESH,
         )
 
-    def value_copy(c, r):
+    def value_copy(h, r):
         return pltpu.make_async_remote_copy(
-            src_ref=v_all.at[0, c],
-            dst_ref=v_all.at[r, c],
-            send_sem=v_send.at[r - 1, c],
-            recv_sem=v_recv.at[r - 1, c],
+            src_ref=v_all.at[0, h],
+            dst_ref=v_all.at[r, h],
+            send_sem=v_send.at[r - 1, h],
+            recv_sem=v_recv.at[r - 1, h],
             device_id=peer(r),
             device_id_type=MESH,
         )
 
-    def slab_to_next(c):
+    def slab_to_next(h):
         return pltpu.make_async_remote_copy(
-            src_ref=pre.at[c, pl.ds(frames - MAXOV, MAXOV)],
-            dst_ref=from_prev.at[c],
-            send_sem=slab_send.at[0, c],
-            recv_sem=slab_recv.at[0, c],
+            src_ref=pre.at[h, pl.ds(frames - MAXOV, MAXOV)],
+            dst_ref=from_prev.at[h],
+            send_sem=slab_send.at[0, h],
+            recv_sem=slab_recv.at[0, h],
             device_id={"window": after},
             device_id_type=MESH,
         )
 
-    def slab_to_prev(c):
+    def slab_to_prev(h):
         return pltpu.make_async_remote_copy(
-            src_ref=pre.at[c, pl.ds(0, MAXOV)],
-            dst_ref=from_next.at[c],
-            send_sem=slab_send.at[1, c],
-            recv_sem=slab_recv.at[1, c],
+            src_ref=pre.at[h, pl.ds(0, MAXOV)],
+            dst_ref=from_next.at[h],
+            send_sem=slab_send.at[1, h],
+            recv_sem=slab_recv.at[1, h],
             device_id={"window": before},
             device_id_type=MESH,
         )
@@ -164,8 +164,19 @@
             key_copy(c, r).start()
 
     def start_values(c):
+        for i in range(HEADS_PER_CHUNK):
+            for r in range(1, peers):
+                value_copy(c * HEADS_PER_CHUNK + i, r).start()
+
+    def finish_sends(c):
         for r in range(1, peers):
-            value_copy(c, r).start()
+            key_copy(c, r).wait_send()
+        for i in range(HEADS_PER_CHUNK):
+            h = c * HEADS_PER_CHUNK + i
+            for r in range(1, peers):
+                value_copy(h, r).wait_send()
+            slab_to_next(h).wait_send()
+            slab_to_prev(h).wait_send()
 
     @pl.loop(0, keys_first)
     def _(c):
@@ -214,9 +225,9 @@
             later[f, :, part] = held + rest
         mean_square = jnp.sum(squares, axis=-1, keepdims=True) * (1.0 / width)
         inv = lax.rsqrt(mean_square + 1e-06)
-        for c in range(chunks):
-            part = pl.ds(c * cols, cols)
-            v_all[0, c, f] = (hidden[:, part] * inv * gain[:, part]).astype(jnp.bfloat16)
+        for h in range(width // depth):
+            part = pl.ds(h * depth, depth)
+            v_all[0, h, f] = (hidden[:, part] * inv * gain[:, part]).astype(jnp.bfloat16)
 
     @pl.loop(0, values_ahead)
     def _(c):
@@ -226,21 +237,22 @@
 
     ov_next = inter[window]
     ov_prev = inter[before]
-    step_next = 1.0 / jnp.full((1, cols), ov_next + 1, jnp.int32).astype(jnp.float32)
-    step_prev = 1.0 / jnp.full((1, cols), ov_prev + 1, jnp.int32).astype(jnp.float32)
-
-    def blend(c):
-        slab_to_next(c).wait_recv()
-        slab_to_prev(c).wait_recv()
+    step_next = 1.0 / jnp.full((1, depth), ov_next + 1, jnp.int32).astype(jnp.float32)
+    step_prev = 1.0 / jnp.full((1, depth), ov_prev + 1, jnp.int32).astype(jnp.float32)
+
+    def blend(h):
+        slab_to_next(h).wait_recv()
+        slab_to_prev(h).wait_recv()
+        here = pl.ds(pl.multiple_of(h * depth, depth), depth)
         for f in range(frames):
-            mine = pre[c, f]
+            mine = pre[h, f]
             if f < MAXOV:
                 inside = jnp.where(f < ov_prev, 1, 0).astype(jnp.float32)
                 ramp = (f + 1.0) * step_prev
-                partner = jnp.zeros((spots, cols), jnp.float32)
+                partner = jnp.zeros((spots, depth), jnp.float32)
                 for s in range(f, MAXOV):
                     hit = jnp.where(MAXOV - ov_prev + f == s, 1, 0).astype(jnp.float32)
-                    partner = partner + hit * from_prev[c, s].astype(jnp.float32)
+                    partner = partner + hit * from_prev[h, s].astype(jnp.float32)
                 share = inside * (1.0 - ramp)
                 mixed = (1.0 - share) * mine.astype(jnp.float32) + share * partner
                 mine = mixed.astype(jnp.bfloat16)
@@ -249,14 +261,14 @@
                 place = g - MAXOV + ov_next
                 inside = jnp.where(place >= 0, 1, 0).astype(jnp.float32)
                 ramp = (place + 1).astype(jnp.float32) * step_next
-                partner = jnp.zeros((spots, cols), jnp.float32)
+                partner = jnp.zeros((spots, depth), jnp.float32)
                 for s in range(g + 1):
                     hit = jnp.where(place == s, 1, 0).astype(jnp.float32)
-                    partner = partner + hit * from_next[c, s].astype(jnp.float32)
+                    partner = partner + hit * from_next[h, s].astype(jnp.float32)
                 share = inside * ramp
                 mixed = (1.0 - share) * mine.astype(jnp.float32) + share * partner
                 mine = mixed.astype(jnp.bfloat16)
-            out_ref[0, f, :, span(c)] = mine
+            out_ref[0, f, :, here] = mine
 
     def weigh(c):
         key_load(c).wait()
@@ -277,19 +289,19 @@
             sums[slot, i] = jnp.broadcast_to(1.0 / summed, (rows, depth))
 
     def attend(c):
-        for r in range(1, peers):
-            value_copy(c, r).wait_recv()
         slot = lax.rem(c, 2)
         for i in range(HEADS_PER_CHUNK):
-            lanes = pl.ds(i * depth, depth)
+            h = c * HEADS_PER_CHUNK + i
+            for r in range(1, peers):
+                value_copy(h, r).wait_recv()
             here = head_span(c, i)
-            head_v = v_all[:, c, :, :, lanes].reshape(peers * rows, depth)
+            head_v = v_all[:, h].reshape(peers * rows, depth)
             total = jnp.dot(probs[slot, i], head_v, preferred_element_type=jnp.float32)
             attended = (total * sums[slot, i]).astype(jnp.bfloat16).astype(jnp.float32)
             mixed = later[:, :, here].reshape(rows, depth) + gate[:, here] * attended
-            pre[c, :, :, lanes] = mixed.astype(jnp.bfloat16).reshape(frames, spots, depth)
-        slab_to_next(c).start()
-        slab_to_prev(c).start()
+            pre[h] = mixed.astype(jnp.bfloat16).reshape(frames, spots, depth)
+            slab_to_next(h).start()
+            slab_to_prev(h).start()
 
     weigh(0)
 
@@ -311,17 +323,13 @@
 
         @pl.when(c >= 1)
         def _():
-            blend(c - 1)
-
-    @pl.loop(0, chunks)
-    def _(c):
-        for r in range(1, peers):
-            key_copy(c, r).wait_send()
-            value_copy(c, r).wait_send()
-        slab_to_next(c).wait_send()
-        slab_to_prev(c).wait_send()
-
-    blend(chunks - 1)
+            for i in range(HEADS_PER_CHUNK):
+                blend((c - 1) * HEADS_PER_CHUNK + i)
+            finish_sends(c - 1)
+
+    for i in range(HEADS_PER_CHUNK):
+        blend((chunks - 1) * HEADS_PER_CHUNK + i)
+    finish_sends(chunks - 1)
 
 
 def on_device(
@@ -356,15 +364,15 @@
         out_specs=vectors,
         scratch_shapes=[
             pltpu.VMEM((peers, chunks, frames, spots, cols), bf16),
-            pltpu.VMEM((peers, chunks, frames, spots, cols), bf16),
+            pltpu.VMEM((peers, heads, frames, spots, depth), bf16),
             pltpu.VMEM((frames, spots, width), bf16),
             pltpu.VMEM((frames, spots, width), bf16),
             pltpu.VMEM((blocks, frames, spots, width), bf16),
             pltpu.VMEM((frames, spots, width), f32),
             pltpu.VMEM((spots, width), f32),
-            pltpu.VMEM((chunks, frames, spots, cols), bf16),
-            pltpu.VMEM((chunks, MAXOV, spots, cols), bf16),
-            pltpu.VMEM((chunks, MAXOV, spots, cols), bf16),
+            pltpu.VMEM((heads, frames, spots, depth), bf16),
+            pltpu.VMEM((heads, MAXOV, spots, depth), bf16),
+            pltpu.VMEM((heads, MAXOV, spots, depth), bf16),
             pltpu.VMEM((2, HEADS_PER_CHUNK, rows, peers * rows), bf16),
             pltpu.VMEM((2, HEADS_PER_CHUNK, rows, depth), f32),
             pltpu.VMEM((1, width), f32),
@@ -377,10 +385,10 @@
             pltpu.SemaphoreType.DMA((6,)),
             pltpu.SemaphoreType.DMA((others, chunks)),
             pltpu.SemaphoreType.DMA((others, chunks)),
-            pltpu.SemaphoreType.DMA((others, chunks)),
-            pltpu.SemaphoreType.DMA((others, chunks)),
-            pltpu.SemaphoreType.DMA((2, chunks)),
-            pltpu.SemaphoreType.DMA((2, chunks)),
+            pltpu.SemaphoreType.DMA((others, heads)),
+            pltpu.SemaphoreType.DMA((others, heads)),
+            pltpu.SemaphoreType.DMA((2, heads)),
+            pltpu.SemaphoreType.DMA((2, heads)),
         ],
         compiler_params=pltpu.CompilerParams(
             collective_id=0, has_side_effects=True, vmem_limit_bytes=56 * 1024 * 1024

time: 76.8 us -> 77.6 us (1.010)
  no operation moved by 1% of the time
where the time goes in v4:
time: 77.6 us; the launch traced here: 77.4 us
  Pallas kernels  76.3 us (98%)
  local copies, waits for them, and re-layouts  1.11 us (1%)
    pallas_call x1, Pallas kernels, on_device(): pl.pallas_call(functools.partial(kernel, peers, windows), out_shape=pltpu...  76.3 us

profile of v4, /device:TPU:0, one launch (start us, length us, event | category | flops | bytes accessed | tf_op | source)
XLA Modules:
  0.0 77.4 jit_solution(4632194468196912260)
XLA Ops:
  0.0 76.3 %shard_map.91 = bf16[1,9,16,5120]{3,2,1,0:T(8,128)(2,1)S(1)} custom-call(bf16[1,9,16,5120]{3,2,1,0:T(8,128)(2,1)} %lat_ref.1, bf16[1,9,16,5120]{3,2,1,0:T(8,128)(2,1)} %q_ref.1, bf16[1,9,16,5120]{3,2,1,0:T(8,128)(2,1)} %k_ref.1, bf16[4,1,9,16,5120]{4,3,2,1,0:T(8,128)(2,1)} %cached_ref.1, s32[4]{0:T(128)} %plan_ref.1, s32[16]{0:T(128)} %refresh_ref.1, ...), custom_call_target="tpu_custom_call" | custom-call | flops 849346560 | bytes 11796480 | tf_op jit(solution)/shard_map/pallas_call | solution.py:360
  76.3 1.1 %copy.11 = bf16[1,9,16,5120]{3,2,1,0:T(8,128)(2,1)} copy(bf16[1,9,16,5120]{3,2,1,0:T(8,128)(2,1)S(1)} %shard_map.91) | data formatting | bytes 2949120

commit v5 on v3

--- a/solution.py
+++ b/solution.py
@@ -11,9 +11,10 @@
 HEAD_DIM = 128
 MAXOV = 4
 HEADS_PER_CHUNK = 2
-KEYS_FIRST = 8
-KEYS_AHEAD = 5
-VALUES_AHEAD = 4
+CHUNKS_PER_GROUP = 2
+KEYS_FIRST = 4
+KEYS_AHEAD = 3
+VALUES_AHEAD = 2
 NORM_COLS = 512
 MESH = pl.DeviceIdType.MESH
 
@@ -64,6 +65,9 @@
     depth = HEAD_DIM
     cols = HEADS_PER_CHUNK * depth
     chunks = width // cols
+    wide = CHUNKS_PER_GROUP * cols
+    groups = width // wide
+    last_chunk = (groups - 1) * CHUNKS_PER_GROUP
     scale = math.log2(math.e) / math.sqrt(depth)
     window = lax.axis_index("window")
     token = lax.axis_index("token")
@@ -73,6 +77,9 @@
     def span(c):
         return pl.ds(pl.multiple_of(c * cols, cols), cols)
 
+    def group_span(g):
+        return pl.ds(pl.multiple_of(g * wide, wide), wide)
+
     def head_span(c, i):
         return pl.ds(pl.multiple_of(c * cols + i * depth, depth), depth)
 
@@ -84,9 +91,9 @@
             cached_ref.at[:, 0, f], cached_own.at[:, f], load_sem.at[1, f]
         )
 
-    def key_load(c):
+    def key_load(g):
         return pltpu.make_async_copy(
-            k_ref.at[0, :, :, span(c)], k_all.at[0, c], key_sem.at[c]
+            k_ref.at[0, :, :, group_span(g)], k_all.at[0, g], key_sem.at[g]
         )
 
     def query_load():
@@ -108,22 +115,34 @@
     def peer(r):
         return {"token": lax.rem(token + r, peers)}
 
-    def key_copy(c, r):
+    def key_copy(g, r):
         return pltpu.make_async_remote_copy(
-            src_ref=k_ref.at[0, :, :, span(c)],
-            dst_ref=k_all.at[r, c],
-            send_sem=k_send.at[r - 1, c],
-            recv_sem=k_recv.at[r - 1, c],
+            src_ref=k_ref.at[0, :, :, group_span(g)],
+            dst_ref=k_all.at[r, g],
+            send_sem=k_send.at[r - 1, g],
+            recv_sem=k_recv.at[r - 1, g],
             device_id=peer(r),
             device_id_type=MESH,
         )
 
-    def value_copy(c, r):
+    def value_copy(g, r):
+        held = pl.ds(g * CHUNKS_PER_GROUP, CHUNKS_PER_GROUP)
+        return pltpu.make_async_remote_copy(
+            src_ref=v_all.at[0, held],
+            dst_ref=v_all.at[r, held],
+            send_sem=v_send.at[r - 1, g],
+            recv_sem=v_recv.at[r - 1, g],
+            device_id=peer(r),
+            device_id_type=MESH,
+        )
+
+    def late_value_copy(c, r):
+        place = groups - 1 + c - last_chunk
         return pltpu.make_async_remote_copy(
             src_ref=v_all.at[0, c],
             dst_ref=v_all.at[r, c],
-            send_sem=v_send.at[r - 1, c],
-            recv_sem=v_recv.at[r - 1, c],
+            send_sem=v_send.at[r - 1, place],
+            recv_sem=v_recv.at[r - 1, place],
             device_id=peer(r),
             device_id_type=MESH,
         )
@@ -156,20 +175,28 @@
 
     pl.semaphore_wait(barrier, peers - 1 + 2)
 
-    keys_first = min(KEYS_FIRST, chunks)
-    values_ahead = min(VALUES_AHEAD, chunks)
-
-    def start_keys(c):
+    keys_first = min(KEYS_FIRST, groups)
+    values_ahead = min(VALUES_AHEAD, groups)
+
+    def start_keys(g):
         for r in range(1, peers):
-            key_copy(c, r).start()
-
-    def start_values(c):
-        for r in range(1, peers):
-            value_copy(c, r).start()
+            key_copy(g, r).start()
+
+    def start_values(g):
+        @pl.when(g < groups - 1)
+        def _():
+            for r in range(1, peers):
+                value_copy(g, r).start()
+
+        @pl.when(g == groups - 1)
+        def _():
+            for j in range(CHUNKS_PER_GROUP):
+                for r in range(1, peers):
+                    late_value_copy(last_chunk + j, r).start()
 
     @pl.loop(0, keys_first)
-    def _(c):
-        start_keys(c)
+    def _(g):
+        start_keys(g)
 
     for load in small_loads:
         load.start()
@@ -181,9 +208,9 @@
 
     query_load().start()
 
-    @pl.loop(0, chunks)
-    def _(c):
-        key_load(c).start()
+    @pl.loop(0, groups)
+    def _(g):
+        key_load(g).start()
 
     for load in small_loads:
         load.wait()
@@ -219,8 +246,8 @@
             v_all[0, c, f] = (hidden[:, part] * inv * gain[:, part]).astype(jnp.bfloat16)
 
     @pl.loop(0, values_ahead)
-    def _(c):
-        start_values(c)
+    def _(g):
+        start_values(g)
 
     query_load().wait()
 
@@ -259,14 +286,20 @@
             out_ref[0, f, :, span(c)] = mine
 
     def weigh(c):
-        key_load(c).wait()
-        for r in range(1, peers):
-            key_copy(c, r).wait_recv()
+        group = c // CHUNKS_PER_GROUP
+        inner = lax.rem(c, CHUNKS_PER_GROUP)
+
+        @pl.when(inner == 0)
+        def _():
+            key_load(group).wait()
+            for r in range(1, peers):
+                key_copy(group, r).wait_recv()
+
         slot = lax.rem(c, 2)
         for i in range(HEADS_PER_CHUNK):
-            lanes = pl.ds(i * depth, depth)
+            lanes = pl.ds(pl.multiple_of(inner * cols + i * depth, depth), depth)
             head_q = q_own[:, :, head_span(c, i)].reshape(rows, depth)
-            head_k = k_all[:, c, :, :, lanes].reshape(peers * rows, depth)
+            head_k = k_all[:, group, :, :, lanes].reshape(peers * rows, depth)
             scores = lax.dot_general(
                 head_q, head_k, (((1,), (1,)), ((), ())), preferred_element_type=jnp.float32
             )
@@ -277,8 +310,16 @@
             sums[slot, i] = jnp.broadcast_to(1.0 / summed, (rows, depth))
 
     def attend(c):
-        for r in range(1, peers):
-            value_copy(c, r).wait_recv()
+        @pl.when(jnp.logical_and(lax.rem(c, CHUNKS_PER_GROUP) == 0, c < last_chunk))
+        def _():
+            for r in range(1, peers):
+                value_copy(c // CHUNKS_PER_GROUP, r).wait_recv()
+
+        @pl.when(c >= last_chunk)
+        def _():
+            for r in range(1, peers):
+                late_value_copy(c, r).wait_recv()
+
         slot = lax.rem(c, 2)
         for i in range(HEADS_PER_CHUNK):
             lanes = pl.ds(i * depth, depth)
@@ -291,17 +332,23 @@
         slab_to_next(c).start()
         slab_to_prev(c).start()
 
-    weigh(0)
+    weigh(jnp.int32(0))
 
     @pl.loop(0, chunks)
     def _(c):
-        @pl.when(c + values_ahead < chunks)
-        def _():
-            start_values(c + values_ahead)
-
-        @pl.when(jnp.logical_and(c + KEYS_AHEAD >= keys_first, c + KEYS_AHEAD < chunks))
-        def _():
-            start_keys(c + KEYS_AHEAD)
+        group = c // CHUNKS_PER_GROUP
+
+        @pl.when(lax.rem(c, CHUNKS_PER_GROUP) == 0)
+        def _():
+            @pl.when(group + values_ahead < groups)
+            def _():
+                start_values(group + values_ahead)
+
+            @pl.when(
+                jnp.logical_and(group + KEYS_AHEAD >= keys_first, group + KEYS_AHEAD < groups)
+            )
+            def _():
+                start_keys(group + KEYS_AHEAD)
 
         attend(c)
 
@@ -312,16 +359,26 @@
         @pl.when(c >= 1)
         def _():
             blend(c - 1)
-
-    @pl.loop(0, chunks)
-    def _(c):
+            slab_to_next(c - 1).wait_send()
+            slab_to_prev(c - 1).wait_send()
+
+    blend(chunks - 1)
+    slab_to_next(chunks - 1).wait_send()
+    slab_to_prev(chunks - 1).wait_send()
+
+    @pl.loop(0, groups)
+    def _(g):
         for r in range(1, peers):
-            key_copy(c, r).wait_send()
-            value_copy(c, r).wait_send()
-        slab_to_next(c).wait_send()
-        slab_to_prev(c).wait_send()
-
-    blend(chunks - 1)
+            key_copy(g, r).wait_send()
+
+    @pl.loop(0, groups - 1)
+    def _(g):
+        for r in range(1, peers):
+            value_copy(g, r).wait_send()
+
+    for j in range(CHUNKS_PER_GROUP):
+        for r in range(1, peers):
+            late_value_copy(last_chunk + j, r).wait_send()
 
 
 def on_device(
@@ -343,6 +400,7 @@
     heads = width // depth
     chunks = heads // HEADS_PER_CHUNK
     cols = HEADS_PER_CHUNK * depth
+    groups = chunks // CHUNKS_PER_GROUP
     rows = frames * spots
     bf16, f32 = jnp.bfloat16, jnp.float32
     in_hbm = pl.BlockSpec(memory_space=pltpu.HBM)
@@ -355,7 +413,7 @@
         in_specs=[in_hbm] * 9,
         out_specs=vectors,
         scratch_shapes=[
-            pltpu.VMEM((peers, chunks, frames, spots, cols), bf16),
+            pltpu.VMEM((peers, groups, frames, spots, CHUNKS_PER_GROUP * cols), bf16),
             pltpu.VMEM((peers, chunks, frames, spots, cols), bf16),
             pltpu.VMEM((frames, spots, width), bf16),
             pltpu.VMEM((frames, spots, width), bf16),
@@ -373,12 +431,12 @@
             pltpu.SMEM(refresh.shape, jnp.int32),
             pltpu.SMEM(intersections.shape, jnp.int32),
             pltpu.SemaphoreType.DMA((2, frames)),
-            pltpu.SemaphoreType.DMA((chunks,)),
+            pltpu.SemaphoreType.DMA((groups,)),
             pltpu.SemaphoreType.DMA((6,)),
-            pltpu.SemaphoreType.DMA((others, chunks)),
-            pltpu.SemaphoreType.DMA((others, chunks)),
-            pltpu.SemaphoreType.DMA((others, chunks)),
-            pltpu.SemaphoreType.DMA((others, chunks)),
+            pltpu.SemaphoreType.DMA((others, groups)),
+            pltpu.SemaphoreType.DMA((others, groups)),
+            pltpu.SemaphoreType.DMA((others, groups + CHUNKS_PER_GROUP - 1)),
+            pltpu.SemaphoreType.DMA((others, groups + CHUNKS_PER_GROUP - 1)),
             pltpu.SemaphoreType.DMA((2, chunks)),
             pltpu.SemaphoreType.DMA((2, chunks)),
         ],

time: 76.8 us -> 76.3 us (level)
  no operation moved by 1% of the time
where the time goes in v5:
time: 76.3 us; the launch traced here: 76.2 us
  Pallas kernels  75.1 us (98%)
  local copies, waits for them, and re-layouts  1.11 us (1%)
    pallas_call x1, Pallas kernels, on_device(): pl.pallas_call(functools.partial(kernel, peers, windows), out_shape=pltpu...  75.1 us

profile of v5, /device:TPU:0, one launch (start us, length us, event | category | flops | bytes accessed | tf_op | source)
XLA Modules:
  0.0 76.2 jit_solution(6002235294312938202)
XLA Ops:
  0.0 75.1 %shard_map.91 = bf16[1,9,16,5120]{3,2,1,0:T(8,128)(2,1)S(1)} custom-call(bf16[1,9,16,5120]{3,2,1,0:T(8,128)(2,1)} %lat_ref.1, bf16[1,9,16,5120]{3,2,1,0:T(8,128)(2,1)} %q_ref.1, bf16[1,9,16,5120]{3,2,1,0:T(8,128)(2,1)} %k_ref.1, bf16[4,1,9,16,5120]{4,3,2,1,0:T(8,128)(2,1)} %cached_ref.1, s32[4]{0:T(128)} %plan_ref.1, s32[16]{0:T(128)} %refresh_ref.1, ...), custom_call_target="tpu_custom_call" | custom-call | flops 849346560 | bytes 11796480 | tf_op jit(solution)/shard_map/pallas_call | solution.py:410
  75.1 1.1 %copy.11 = bf16[1,9,16,5120]{3,2,1,0:T(8,128)(2,1)} copy(bf16[1,9,16,5120]{3,2,1,0:T(8,128)(2,1)S(1)} %shard_map.91) | data formatting | bytes 2949120

commit v6 on v5

--- a/solution.py
+++ b/solution.py
@@ -362,10 +362,6 @@
             slab_to_next(c - 1).wait_send()
             slab_to_prev(c - 1).wait_send()
 
-    blend(chunks - 1)
-    slab_to_next(chunks - 1).wait_send()
-    slab_to_prev(chunks - 1).wait_send()
-
     @pl.loop(0, groups)
     def _(g):
         for r in range(1, peers):
@@ -379,6 +375,20 @@
     for j in range(CHUNKS_PER_GROUP):
         for r in range(1, peers):
             late_value_copy(last_chunk + j, r).wait_send()
+    slab_to_next(chunks - 1).wait_send()
+    slab_to_prev(chunks - 1).wait_send()
+    blend(chunks - 1)
+
+
+def store(held_ref, out_ref, sem):
+    copies = [
+        pltpu.make_async_copy(held_ref.at[:, f], out_ref.at[:, f], sem.at[f])
+        for f in range(held_ref.shape[1])
+    ]
+    for copy in copies:
+        copy.start()
+    for copy in copies:
+        copy.wait()
 
 
 def on_device(
@@ -407,7 +417,7 @@
     vectors = pl.BlockSpec(memory_space=pltpu.VMEM)
     others = max(peers - 1, 1)
     flops = 4 * rows * rows * peers * width
-    return pl.pallas_call(
+    blended = pl.pallas_call(
         functools.partial(kernel, peers, windows),
         out_shape=pltpu.VMEM(latents.shape, bf16),
         in_specs=[in_hbm] * 9,
@@ -459,6 +469,13 @@
         attn_gate.reshape(1, width),
         intersections,
     )
+    return pl.pallas_call(
+        store,
+        out_shape=jax.ShapeDtypeStruct(latents.shape, bf16),
+        in_specs=[pl.BlockSpec(memory_space=pl.ANY)],
+        out_specs=pl.BlockSpec(memory_space=pltpu.HBM),
+        scratch_shapes=[pltpu.SemaphoreType.DMA((frames,))],
+    )(blended)
 
 
 def solution(mesh):

time: 76.3 us -> 122 us (1.60)
  Pallas kernels: 75.1 us -> 121 us
    pallas_call x0 -> x1, Pallas kernels: none -> 45.8 us  [on_device(): pl.pallas_call(store, out_shape=jax.ShapeDtypeStruct(latents.shape, bf16)...]
where the time goes in v6:
time: 122 us
  Pallas kernels  121 us (99%)
    pallas_call x1, Pallas kernels, on_device(): pl.pallas_call(functools.partial(kernel, peers, windows), out_shape=pltpu...  74.9 us
    pallas_call x1, Pallas kernels, on_device(): pl.pallas_call(store, out_shape=jax.ShapeDtypeStruct(latents.shape, bf16)...  45.8 us

profile of v6, /device:TPU:0, one launch (start us, length us, event | category | flops | bytes accessed | tf_op | source)
XLA Modules:
  0.0 122.0 jit_solution(5735107670090020172)
XLA Ops:
  0.0 74.9 %shard_map.91.held_ref = bf16[1,9,16,5120]{3,2,1,0:T(8,128)(2,1)S(1)} custom-call(bf16[1,9,16,5120]{3,2,1,0:T(8,128)(2,1)} %lat_ref.1, bf16[1,9,16,5120]{3,2,1,0:T(8,128)(2,1)} %q_ref.1, bf16[1,9,16,5120]{3,2,1,0:T(8,128)(2,1)} %k_ref.1, bf16[4,1,9,16,5120]{4,3,2,1,0:T(8,128)(2,1)} %cached_ref.1, s32[4]{0:T(128)} %plan_ref.1, s32[16]{0:T(128)} %refresh_ref.1, ...), custom_call_target="tpu_custom_call" | custom-call | flops 849346560 | bytes 11796480 | tf_op jit(solution)/shard_map/pallas_call | solution.py:420
  75.0 0.0 copy-start
  75.0 1.1 copy-done
  76.1 45.8 %shard_map.92 = bf16[1,9,16,5120]{3,2,1,0:T(8,128)(2,1)} custom-call(bf16[1,9,16,5120]{3,2,1,0:T(8,128)(2,1)} %copy-done), custom_call_target="tpu_custom_call" | custom-call | tf_op jit(solution)/shard_map/pallas_call | solution.py:472
Async XLA Ops:
  75.0 1.2 copy-start

commit v7 on v5

--- a/solution.py
+++ b/solution.py
@@ -125,47 +125,55 @@
             device_id_type=MESH,
         )
 
-    def value_copy(g, r):
-        held = pl.ds(g * CHUNKS_PER_GROUP, CHUNKS_PER_GROUP)
+    def value_piece(held, place, r):
         return pltpu.make_async_remote_copy(
             src_ref=v_all.at[0, held],
             dst_ref=v_all.at[r, held],
-            send_sem=v_send.at[r - 1, g],
-            recv_sem=v_recv.at[r - 1, g],
-            device_id=peer(r),
-            device_id_type=MESH,
-        )
-
-    def late_value_copy(c, r):
-        place = groups - 1 + c - last_chunk
-        return pltpu.make_async_remote_copy(
-            src_ref=v_all.at[0, c],
-            dst_ref=v_all.at[r, c],
             send_sem=v_send.at[r - 1, place],
             recv_sem=v_recv.at[r - 1, place],
             device_id=peer(r),
             device_id_type=MESH,
         )
 
-    def slab_to_next(c):
+    def value_copy(g, r):
+        count = CHUNKS_PER_GROUP * HEADS_PER_CHUNK
+        return value_piece(pl.ds(g * count, count), g, r)
+
+    def late_value_copy(c, r):
+        held = pl.ds(c * HEADS_PER_CHUNK, HEADS_PER_CHUNK)
+        return value_piece(held, groups - 1 + c - last_chunk, r)
+
+    def end_value_copy(i, r):
+        held = pl.ds((chunks - 1) * HEADS_PER_CHUNK + i, 1)
+        return value_piece(held, groups + CHUNKS_PER_GROUP - 2 + i, r)
+
+    def slab_to_next(held, place):
         return pltpu.make_async_remote_copy(
-            src_ref=pre.at[c, pl.ds(frames - MAXOV, MAXOV)],
-            dst_ref=from_prev.at[c],
-            send_sem=slab_send.at[0, c],
-            recv_sem=slab_recv.at[0, c],
+            src_ref=pre.at[held, pl.ds(frames - MAXOV, MAXOV)],
+            dst_ref=from_prev.at[held],
+            send_sem=slab_send.at[0, place],
+            recv_sem=slab_recv.at[0, place],
             device_id={"window": after},
             device_id_type=MESH,
         )
 
-    def slab_to_prev(c):
+    def slab_to_prev(held, place):
         return pltpu.make_async_remote_copy(
-            src_ref=pre.at[c, pl.ds(0, MAXOV)],
-            dst_ref=from_next.at[c],
-            send_sem=slab_send.at[1, c],
-            recv_sem=slab_recv.at[1, c],
+            src_ref=pre.at[held, pl.ds(0, MAXOV)],
+            dst_ref=from_next.at[held],
+            send_sem=slab_send.at[1, place],
+            recv_sem=slab_recv.at[1, place],
             device_id={"window": before},
             device_id_type=MESH,
         )
+
+    def slabs(c):
+        held = pl.ds(c * HEADS_PER_CHUNK, HEADS_PER_CHUNK)
+        return slab_to_next(held, c), slab_to_prev(held, c)
+
+    def end_slabs(i):
+        held = pl.ds((chunks - 1) * HEADS_PER_CHUNK + i, 1)
+        return slab_to_next(held, chunks - 1 + i), slab_to_prev(held, chunks - 1 + i)
 
     barrier = pltpu.get_barrier_semaphore()
     for r in range(1, peers):
@@ -190,9 +198,12 @@
 
         @pl.when(g == groups - 1)
         def _():
-            for j in range(CHUNKS_PER_GROUP):
+            for j in range(CHUNKS_PER_GROUP - 1):
                 for r in range(1, peers):
                     late_value_copy(last_chunk + j, r).start()
+            for i in range(HEADS_PER_CHUNK):
+                for r in range(1, peers):
+                    end_value_copy(i, r).start()
 
     @pl.loop(0, keys_first)
     def _(g):
@@ -241,9 +252,9 @@
             later[f, :, part] = held + rest
         mean_square = jnp.sum(squares, axis=-1, keepdims=True) * (1.0 / width)
         inv = lax.rsqrt(mean_square + 1e-06)
-        for c in range(chunks):
-            part = pl.ds(c * cols, cols)
-            v_all[0, c, f] = (hidden[:, part] * inv * gain[:, part]).astype(jnp.bfloat16)
+        for h in range(width // depth):
+            part = pl.ds(h * depth, depth)
+            v_all[0, h, f] = (hidden[:, part] * inv * gain[:, part]).astype(jnp.bfloat16)
 
     @pl.loop(0, values_ahead)
     def _(g):
@@ -253,21 +264,20 @@
 
     ov_next = inter[window]
     ov_prev = inter[before]
-    step_next = 1.0 / jnp.full((1, cols), ov_next + 1, jnp.int32).astype(jnp.float32)
-    step_prev = 1.0 / jnp.full((1, cols), ov_prev + 1, jnp.int32).astype(jnp.float32)
-
-    def blend(c):
-        slab_to_next(c).wait_recv()
-        slab_to_prev(c).wait_recv()
+    step_next = 1.0 / jnp.full((1, depth), ov_next + 1, jnp.int32).astype(jnp.float32)
+    step_prev = 1.0 / jnp.full((1, depth), ov_prev + 1, jnp.int32).astype(jnp.float32)
+
+    def blend(h):
+        here = pl.ds(pl.multiple_of(h * depth, depth), depth)
         for f in range(frames):
-            mine = pre[c, f]
+            mine = pre[h, f]
             if f < MAXOV:
                 inside = jnp.where(f < ov_prev, 1, 0).astype(jnp.float32)
                 ramp = (f + 1.0) * step_prev
-                partner = jnp.zeros((spots, cols), jnp.float32)
+                partner = jnp.zeros((spots, depth), jnp.float32)
                 for s in range(f, MAXOV):
                     hit = jnp.where(MAXOV - ov_prev + f == s, 1, 0).astype(jnp.float32)
-                    partner = partner + hit * from_prev[c, s].astype(jnp.float32)
+                    partner = partner + hit * from_prev[h, s].astype(jnp.float32)
                 share = inside * (1.0 - ramp)
                 mixed = (1.0 - share) * mine.astype(jnp.float32) + share * partner
                 mine = mixed.astype(jnp.bfloat16)
@@ -276,14 +286,14 @@
                 place = g - MAXOV + ov_next
                 inside = jnp.where(place >= 0, 1, 0).astype(jnp.float32)
                 ramp = (place + 1).astype(jnp.float32) * step_next
-                partner = jnp.zeros((spots, cols), jnp.float32)
+                partner = jnp.zeros((spots, depth), jnp.float32)
                 for s in range(g + 1):
                     hit = jnp.where(place == s, 1, 0).astype(jnp.float32)
-                    partner = partner + hit * from_next[c, s].astype(jnp.float32)
+                    partner = partner + hit * from_next[h, s].astype(jnp.float32)
                 share = inside * ramp
                 mixed = (1.0 - share) * mine.astype(jnp.float32) + share * partner
                 mine = mixed.astype(jnp.bfloat16)
-            out_ref[0, f, :, span(c)] = mine
+            out_ref[0, f, :, here] = mine
 
     def weigh(c):
         group = c // CHUNKS_PER_GROUP
@@ -309,32 +319,19 @@
             probs[slot, i] = weights.astype(jnp.bfloat16)
             sums[slot, i] = jnp.broadcast_to(1.0 / summed, (rows, depth))
 
-    def attend(c):
-        @pl.when(jnp.logical_and(lax.rem(c, CHUNKS_PER_GROUP) == 0, c < last_chunk))
-        def _():
-            for r in range(1, peers):
-                value_copy(c // CHUNKS_PER_GROUP, r).wait_recv()
-
-        @pl.when(c >= last_chunk)
-        def _():
-            for r in range(1, peers):
-                late_value_copy(c, r).wait_recv()
-
+    def attend(c, i):
         slot = lax.rem(c, 2)
-        for i in range(HEADS_PER_CHUNK):
-            lanes = pl.ds(i * depth, depth)
-            here = head_span(c, i)
-            head_v = v_all[:, c, :, :, lanes].reshape(peers * rows, depth)
-            total = jnp.dot(probs[slot, i], head_v, preferred_element_type=jnp.float32)
-            attended = (total * sums[slot, i]).astype(jnp.bfloat16).astype(jnp.float32)
-            mixed = later[:, :, here].reshape(rows, depth) + gate[:, here] * attended
-            pre[c, :, :, lanes] = mixed.astype(jnp.bfloat16).reshape(frames, spots, depth)
-        slab_to_next(c).start()
-        slab_to_prev(c).start()
+        h = c * HEADS_PER_CHUNK + i
+        here = head_span(c, i)
+        head_v = v_all[:, h].reshape(peers * rows, depth)
+        total = jnp.dot(probs[slot, i], head_v, preferred_element_type=jnp.float32)
+        attended = (total * sums[slot, i]).astype(jnp.bfloat16).astype(jnp.float32)
+        mixed = later[:, :, here].reshape(rows, depth) + gate[:, here] * attended
+        pre[h] = mixed.astype(jnp.bfloat16).reshape(frames, spots, depth)
 
     weigh(jnp.int32(0))
 
-    @pl.loop(0, chunks)
+    @pl.loop(0, chunks - 1)
     def _(c):
         group = c // CHUNKS_PER_GROUP
 
@@ -350,21 +347,45 @@
             def _():
                 start_keys(group + KEYS_AHEAD)
 
-        attend(c)
-
-        @pl.when(c + 1 < chunks)
-        def _():
-            weigh(c + 1)
+        @pl.when(jnp.logical_and(lax.rem(c, CHUNKS_PER_GROUP) == 0, c < last_chunk))
+        def _():
+            for r in range(1, peers):
+                value_copy(group, r).wait_recv()
+
+        @pl.when(c >= last_chunk)
+        def _():
+            for r in range(1, peers):
+                late_value_copy(c, r).wait_recv()
+
+        for i in range(HEADS_PER_CHUNK):
+            attend(c, i)
+        for slab in slabs(c):
+            slab.start()
+
+        weigh(c + 1)
 
         @pl.when(c >= 1)
         def _():
-            blend(c - 1)
-            slab_to_next(c - 1).wait_send()
-            slab_to_prev(c - 1).wait_send()
-
-    blend(chunks - 1)
-    slab_to_next(chunks - 1).wait_send()
-    slab_to_prev(chunks - 1).wait_send()
+            for slab in slabs(c - 1):
+                slab.wait()
+            for i in range(HEADS_PER_CHUNK):
+                blend((c - 1) * HEADS_PER_CHUNK + i)
+
+    end = chunks - 1
+    for i in range(HEADS_PER_CHUNK):
+        for r in range(1, peers):
+            end_value_copy(i, r).wait_recv()
+        attend(jnp.int32(end), i)
+        for slab in end_slabs(i):
+            slab.start()
+    for slab in slabs(end - 1):
+        slab.wait()
+    for i in range(HEADS_PER_CHUNK):
+        blend((end - 1) * HEADS_PER_CHUNK + i)
+    for i in range(HEADS_PER_CHUNK):
+        for slab in end_slabs(i):
+            slab.wait()
+        blend(end * HEADS_PER_CHUNK + i)
 
     @pl.loop(0, groups)
     def _(g):
@@ -376,9 +397,11 @@
         for r in range(1, peers):
             value_copy(g, r).wait_send()
 
-    for j in range(CHUNKS_PER_GROUP):
-        for r in range(1, peers):
+    for r in range(1, peers):
+        for j in range(CHUNKS_PER_GROUP - 1):
             late_value_copy(last_chunk + j, r).wait_send()
+        for i in range(HEADS_PER_CHUNK):
+            end_value_copy(i, r).wait_send()
 
 
 def on_device(
@@ -401,6 +424,7 @@
     chunks = heads // HEADS_PER_CHUNK
     cols = HEADS_PER_CHUNK * depth
     groups = chunks // CHUNKS_PER_GROUP
+    places = groups + CHUNKS_PER_GROUP + HEADS_PER_CHUNK - 2
     rows = frames * spots
     bf16, f32 = jnp.bfloat16, jnp.float32
     in_hbm = pl.BlockSpec(memory_space=pltpu.HBM)
@@ -414,15 +438,15 @@
         out_specs=vectors,
         scratch_shapes=[
             pltpu.VMEM((peers, groups, frames, spots, CHUNKS_PER_GROUP * cols), bf16),
-            pltpu.VMEM((peers, chunks, frames, spots, cols), bf16),
+            pltpu.VMEM((peers, heads, frames, spots, depth), bf16),
             pltpu.VMEM((frames, spots, width), bf16),
             pltpu.VMEM((frames, spots, width), bf16),
             pltpu.VMEM((blocks, frames, spots, width), bf16),
             pltpu.VMEM((frames, spots, width), f32),
             pltpu.VMEM((spots, width), f32),
-            pltpu.VMEM((chunks, frames, spots, cols), bf16),
-            pltpu.VMEM((chunks, MAXOV, spots, cols), bf16),
-            pltpu.VMEM((chunks, MAXOV, spots, cols), bf16),
+            pltpu.VMEM((heads, frames, spots, depth), bf16),
+            pltpu.VMEM((heads, MAXOV, spots, depth), bf16),
+            pltpu.VMEM((heads, MAXOV, spots, depth), bf16),
             pltpu.VMEM((2, HEADS_PER_CHUNK, rows, peers * rows), bf16),
             pltpu.VMEM((2, HEADS_PER_CHUNK, rows, depth), f32),
             pltpu.VMEM((1, width), f32),
@@ -435,10 +459,10 @@
             pltpu.SemaphoreType.DMA((6,)),
             pltpu.SemaphoreType.DMA((others, groups)),
             pltpu.SemaphoreType.DMA((others, groups)),
-            pltpu.SemaphoreType.DMA((others, groups + CHUNKS_PER_GROUP - 1)),
-            pltpu.SemaphoreType.DMA((others, groups + CHUNKS_PER_GROUP - 1)),
-            pltpu.SemaphoreType.DMA((2, chunks)),
-            pltpu.SemaphoreType.DMA((2, chunks)),
+            pltpu.SemaphoreType.DMA((others, places)),
+            pltpu.SemaphoreType.DMA((others, places)),
+            pltpu.SemaphoreType.DMA((2, chunks + HEADS_PER_CHUNK - 1)),
+            pltpu.SemaphoreType.DMA((2, chunks + HEADS_PER_CHUNK - 1)),
         ],
         compiler_params=pltpu.CompilerParams(
             collective_id=0, has_side_effects=True, vmem_limit_bytes=56 * 1024 * 1024

time: 76.3 us -> 76.2 us (level)
  no operation moved by 1% of the time
where the time goes in v7:
time: 76.2 us; the launch traced here: 76.1 us
  Pallas kernels  75 us (98%)
  local copies, waits for them, and re-layouts  1.11 us (1%)
    pallas_call x1, Pallas kernels, on_device(): pl.pallas_call(functools.partial(kernel, peers, windows), out_shape=pltpu...  75 us

profile of v7, /device:TPU:0, one launch (start us, length us, event | category | flops | bytes accessed | tf_op | source)
XLA Modules:
  0.0 76.1 jit_solution(8009669467097429789)
XLA Ops:
  0.0 75.0 %shard_map.91 = bf16[1,9,16,5120]{3,2,1,0:T(8,128)(2,1)S(1)} custom-call(bf16[1,9,16,5120]{3,2,1,0:T(8,128)(2,1)} %lat_ref.1, bf16[1,9,16,5120]{3,2,1,0:T(8,128)(2,1)} %q_ref.1, bf16[1,9,16,5120]{3,2,1,0:T(8,128)(2,1)} %k_ref.1, bf16[4,1,9,16,5120]{4,3,2,1,0:T(8,128)(2,1)} %cached_ref.1, s32[4]{0:T(128)} %plan_ref.1, s32[16]{0:T(128)} %refresh_ref.1, ...), custom_call_target="tpu_custom_call" | custom-call | flops 849346560 | bytes 11796480 | tf_op jit(solution)/shard_map/pallas_call | solution.py:434
  75.0 1.1 %copy.11 = bf16[1,9,16,5120]{3,2,1,0:T(8,128)(2,1)} copy(bf16[1,9,16,5120]{3,2,1,0:T(8,128)(2,1)S(1)} %shard_map.91) | data formatting | bytes 2949120

commit v8 on v7

--- a/solution.py
+++ b/solution.py
@@ -12,7 +12,8 @@
 MAXOV = 4
 HEADS_PER_CHUNK = 2
 CHUNKS_PER_GROUP = 2
-KEYS_FIRST = 4
+KEYS_FIRST = 5
+KEYS_HELD = 1
 KEYS_AHEAD = 3
 VALUES_AHEAD = 2
 NORM_COLS = 512
@@ -205,9 +206,13 @@
                 for r in range(1, peers):
                     end_value_copy(i, r).start()
 
+    held_back = jnp.logical_or(window == 1, window == windows - 2)
+
     @pl.loop(0, keys_first)
     def _(g):
-        start_keys(g)
+        @pl.when(jnp.logical_or(g < KEYS_HELD, jnp.logical_not(held_back)))
+        def _():
+            start_keys(g)
 
     for load in small_loads:
         load.start()
@@ -255,6 +260,12 @@
         for h in range(width // depth):
             part = pl.ds(h * depth, depth)
             v_all[0, h, f] = (hidden[:, part] * inv * gain[:, part]).astype(jnp.bfloat16)
+
+    @pl.loop(KEYS_HELD, keys_first)
+    def _(g):
+        @pl.when(held_back)
+        def _():
+            start_keys(g)
 
     @pl.loop(0, values_ahead)
     def _(g):

time: 76.2 us -> 77.6 us (1.018)
  Pallas kernels: 75 us -> 76.3 us
    pallas_call x1, Pallas kernels: 75 us -> 76.3 us  [on_device(): pl.pallas_call(functools.partial(kernel, peers, windows), out_shape=pltpu...]
where the time goes in v8:
time: 77.6 us; the launch traced here: 77.4 us
  Pallas kernels  76.3 us (98%)
  local copies, waits for them, and re-layouts  1.11 us (1%)
    pallas_call x1, Pallas kernels, on_device(): pl.pallas_call(functools.partial(kernel, peers, windows), out_shape=pltpu...  76.3 us

profile of v8, /device:TPU:0, one launch (start us, length us, event | category | flops | bytes accessed | tf_op | source)
XLA Modules:
  0.0 77.4 jit_solution(2873176102332896165)
XLA Ops:
  0.0 76.3 %shard_map.91 = bf16[1,9,16,5120]{3,2,1,0:T(8,128)(2,1)S(1)} custom-call(bf16[1,9,16,5120]{3,2,1,0:T(8,128)(2,1)} %lat_ref.1, bf16[1,9,16,5120]{3,2,1,0:T(8,128)(2,1)} %q_ref.1, bf16[1,9,16,5120]{3,2,1,0:T(8,128)(2,1)} %k_ref.1, bf16[4,1,9,16,5120]{4,3,2,1,0:T(8,128)(2,1)} %cached_ref.1, s32[4]{0:T(128)} %plan_ref.1, s32[16]{0:T(128)} %refresh_ref.1, ...), custom_call_target="tpu_custom_call" | custom-call | flops 849346560 | bytes 11796480 | tf_op jit(solution)/shard_map/pallas_call | solution.py:445
  76.3 1.1 %copy.11 = bf16[1,9,16,5120]{3,2,1,0:T(8,128)(2,1)} copy(bf16[1,9,16,5120]{3,2,1,0:T(8,128)(2,1)S(1)} %shard_map.91) | data formatting | bytes 2949120

commit v9 on v8

--- a/solution.py
+++ b/solution.py
@@ -206,7 +206,7 @@
                 for r in range(1, peers):
                     end_value_copy(i, r).start()
 
-    held_back = jnp.logical_or(window == 1, window == windows - 2)
+    held_back = window == windows - 2
 
     @pl.loop(0, keys_first)
     def _(g):

time: 77.6 us -> 77.4 us (level)
  no operation moved by 1% of the time
where the time goes in v9:
time: 77.4 us; the launch traced here: 77.2 us
  Pallas kernels  76.1 us (98%)
  local copies, waits for them, and re-layouts  1.11 us (1%)
    pallas_call x1, Pallas kernels, on_device(): pl.pallas_call(functools.partial(kernel, peers, windows), out_shape=pltpu...  76.1 us

profile of v9, /device:TPU:0, one launch (start us, length us, event | category | flops | bytes accessed | tf_op | source)
XLA Modules:
  0.0 77.2 jit_solution(13831994954861489863)
XLA Ops:
  0.0 76.1 %shard_map.91 = bf16[1,9,16,5120]{3,2,1,0:T(8,128)(2,1)S(1)} custom-call(bf16[1,9,16,5120]{3,2,1,0:T(8,128)(2,1)} %lat_ref.1, bf16[1,9,16,5120]{3,2,1,0:T(8,128)(2,1)} %q_ref.1, bf16[1,9,16,5120]{3,2,1,0:T(8,128)(2,1)} %k_ref.1, bf16[4,1,9,16,5120]{4,3,2,1,0:T(8,128)(2,1)} %cached_ref.1, s32[4]{0:T(128)} %plan_ref.1, s32[16]{0:T(128)} %refresh_ref.1, ...), custom_call_target="tpu_custom_call" | custom-call | flops 849346560 | bytes 11796480 | tf_op jit(solution)/shard_map/pallas_call | solution.py:445
  76.1 1.1 %copy.11 = bf16[1,9,16,5120]{3,2,1,0:T(8,128)(2,1)} copy(bf16[1,9,16,5120]{3,2,1,0:T(8,128)(2,1)S(1)} %shard_map.91) | data formatting | bytes 2949120
